TPU v7x, 512 devices: a whole 4x4x16 slice. The times are simulated.
512 devices in a mesh: dp: 32 (over x, z_lo, core), seq: 16 (over y, z_hi).
Axes of the slice: x: 4, y: 4, z: 16 (z_hi: 4, z_lo: 4; z = z_hi * 4 + z_lo), core: 2. Of those that a mesh axis runs over, the one named last changes fastest.
Arguments:
- query: bfloat16 [32, 2048, 2048], P('dp', 'seq'), may hold values from -6 to 6
- key: bfloat16 [32, 2048, 2048], P('dp', 'seq'), may hold values from -6 to 6
- value: bfloat16 [32, 2048, 2048], P('dp', 'seq'), may hold values from -6 to 6
- patch_map: int32 [32, 2048], P('dp', 'seq'), may hold values from 0 to 127, as said below
- teacher: bfloat16 [32, 128, 1408], P('dp', 'seq'), may hold values from -6 to 6
- proj_in: bfloat16 [2048, 2048], P(None, 'seq'), may hold values from -0.13258252 to 0.13258252
- proj_out: bfloat16 [2048, 1408], P('seq'), may hold values from -0.13258252 to 0.13258252
Outputs:
- grad_query: bfloat16 [32, 2048, 2048], P('dp', 'seq')
- grad_value: bfloat16 [32, 2048, 2048], P('dp', 'seq')
- grad_in: float32 [2048, 2048], P(None, 'seq')
- grad_out: float32 [2048, 1408], P('seq')
Inputs may be any that keep to these rules, and one draw needn't show every extreme that they name: `patch_map`: each teacher patch of a clip is named by exactly 16 of that clip's tokens.
All inputs are finite; a program needn't handle non-finite values.
Results may differ from a plain program's by a relative error of at most 0.02.
Values may be sent and summed in bfloat16 or wider, within the bound.
No kernel may reach another device: no remote copies, remote signals or barrier semaphores. Data moves between devices by JAX's collectives and lax.ppermute only.
A program may use at most 64 MiB of HBM per device.

v0:
```python
import jax
import jax.numpy as jnp
from jax import lax
from jax.sharding import PartitionSpec as P

HEAD_DIM = 64


SCALE = 0.125
EPSILON = 1e-06


def block_rows():
    return 512


def block_probs(query_rows, key_heads):
    scores = (
        jnp.einsum("qhd,khd->hqk", query_rows, key_heads, preferred_element_type=jnp.float32)
        * SCALE
    )
    highest = jnp.max(scores, axis=-1, keepdims=True)
    weights = jnp.exp(scores - highest)
    return (weights / jnp.sum(weights, axis=-1, keepdims=True)).astype(jnp.bfloat16)


def attention_forward(query_heads, key_heads, value_heads):
    length, heads_here, head_size = query_heads.shape
    size = block_rows()

    def step(carried, position):
        query_rows = lax.dynamic_slice_in_dim(query_heads, position * size, size, 0)
        weights = block_probs(query_rows, key_heads)
        result = jnp.einsum(
            "hqk,khd->qhd", weights, value_heads, preferred_element_type=jnp.float32
        )
        return (carried, result.astype(jnp.bfloat16))

    carried, blocks = lax.scan(step, 0, jnp.arange(length // size))
    return blocks.reshape(length, heads_here * head_size)


def attention_backward(query_heads, key_heads, value_heads, grad_heads):
    length, heads_here, head_size = query_heads.shape
    size = block_rows()

    def step(grad_values, position):
        query_rows = lax.dynamic_slice_in_dim(query_heads, position * size, size, 0)
        upstream = lax.dynamic_slice_in_dim(grad_heads, position * size, size, 0)
        weights = block_probs(query_rows, key_heads)
        grad_values = grad_values + jnp.einsum(
            "hqk,qhd->khd", weights, upstream, preferred_element_type=jnp.float32
        )
        dprob = jnp.einsum(
            "qhd,khd->hqk", upstream, value_heads, preferred_element_type=jnp.float32
        )
        weights_f = weights.astype(jnp.float32)
        delta = jnp.sum(weights_f * dprob, axis=-1, keepdims=True)
        dscore = (weights_f * (dprob - delta) * SCALE).astype(jnp.bfloat16)
        grad_rows = jnp.einsum(
            "hqk,khd->qhd", dscore, key_heads, preferred_element_type=jnp.float32
        )
        return (grad_values, grad_rows.astype(jnp.bfloat16))

    start = jnp.zeros((length, heads_here, head_size), jnp.float32)
    grad_values, blocks = lax.scan(step, start, jnp.arange(length // size))
    grad_queries = blocks.reshape(length, heads_here * head_size)
    return (grad_queries, grad_values.astype(jnp.bfloat16).reshape(length, heads_here * head_size))


def per_device(query, key, value, patch_map, teacher, proj_in, proj_out):
    query_ex, key_ex, value_ex = (
        lax.all_to_all(query, "seq", split_axis=2, concat_axis=1, tiled=True),
        lax.all_to_all(key, "seq", split_axis=2, concat_axis=1, tiled=True),
        lax.all_to_all(value, "seq", split_axis=2, concat_axis=1, tiled=True),
    )
    seq_length = query_ex.shape[1]
    head_width = query_ex.shape[2]
    heads_here = head_width // HEAD_DIM
    query_heads = query_ex[0].reshape(seq_length, heads_here, HEAD_DIM)
    key_heads = key_ex[0].reshape(seq_length, heads_here, HEAD_DIM)
    value_heads = value_ex[0].reshape(seq_length, heads_here, HEAD_DIM)
    attended = attention_forward(query_heads, key_heads, value_heads)
    patch_count = teacher.shape[1] * lax.axis_size("seq")
    group_size = query.shape[1] // teacher.shape[1]
    patch_range = jnp.arange(patch_count, dtype=jnp.int32)
    token_rows = lax.all_to_all(attended[None], "seq", split_axis=1, concat_axis=2, tiled=True)[0]
    selector = (patch_map[0][None, :] == patch_range[:, None]).astype(jnp.bfloat16)
    pooled_sum = lax.psum(jnp.dot(selector, token_rows, preferred_element_type=jnp.float32), "seq")
    pooled = (pooled_sum / group_size).astype(jnp.bfloat16)
    preact = jnp.dot(pooled, proj_in, preferred_element_type=jnp.float32)
    hidden = jax.nn.silu(preact).astype(jnp.bfloat16)
    partial_proj = jnp.dot(hidden, proj_out, preferred_element_type=jnp.float32)
    proj = lax.psum_scatter(partial_proj, "seq", scatter_dimension=0, tiled=True)
    target = teacher[0].astype(jnp.float32)
    cross_term = jnp.mean(proj * target, axis=-1, keepdims=True)
    proj_power = jnp.mean(proj * proj, axis=-1, keepdims=True) + EPSILON
    teach_power = jnp.mean(target * target, axis=-1, keepdims=True) + EPSILON
    grad_rows = (
        -(target - cross_term / proj_power * proj) / jnp.sqrt(proj_power * teach_power)
    ).astype(jnp.bfloat16)
    grad_proj = lax.all_gather(grad_rows, "seq", axis=0, tiled=True)
    grad_out_local = jnp.dot(hidden.T, grad_proj, preferred_element_type=jnp.float32)
    grad_hidden = jnp.dot(grad_proj, proj_out.T, preferred_element_type=jnp.float32)
    sigma = jax.nn.sigmoid(preact)
    grad_pre = (grad_hidden * sigma * (1.0 + preact * (1.0 - sigma))).astype(jnp.bfloat16)
    grad_in_local = jnp.dot(pooled.T, grad_pre, preferred_element_type=jnp.float32)
    pooled_terms = jnp.dot(grad_pre, proj_in.T, preferred_element_type=jnp.float32)
    grad_pooled = lax.psum(pooled_terms, "seq").astype(jnp.bfloat16)
    grad_tokens = (
        jnp.dot(selector.T, grad_pooled, preferred_element_type=jnp.float32) / group_size
    ).astype(jnp.bfloat16)
    grad_attended = lax.all_to_all(
        grad_tokens[None], "seq", split_axis=2, concat_axis=1, tiled=True
    )[0]
    grad_heads = grad_attended.reshape(seq_length, heads_here, HEAD_DIM)
    grad_queries, grad_values = attention_backward(query_heads, key_heads, value_heads, grad_heads)
    grad_query, grad_value = (
        lax.all_to_all(grad_queries[None], "seq", split_axis=1, concat_axis=2, tiled=True),
        lax.all_to_all(grad_values[None], "seq", split_axis=1, concat_axis=2, tiled=True),
    )
    grad_in_total, grad_out_total = lax.psum((grad_in_local, grad_out_local), "dp")
    return (grad_query, grad_value, grad_in_total, grad_out_total)


def solution(mesh):
    placed = (
        P("dp", "seq", None),
        P("dp", "seq", None),
        P("dp", "seq", None),
        P("dp", "seq"),
        P("dp", "seq", None),
        P(None, "seq"),
        P("seq", None),
    )
    return jax.shard_map(
        per_device,
        mesh=mesh,
        in_specs=placed,
        out_specs=(P("dp", "seq", None), P("dp", "seq", None), P(None, "seq"), P("seq", None)),
        check_vma=False,
    )
```

profile of v0, /device:TPU:1, one launch (start us, length us, event | category | flops | bytes accessed | tf_op | source)
XLA Modules:
  0.0 1402.7 jit_solution(6201970802147004495)
XLA Ops:
  10.2 11.5 reduce
  22.6 18.4 %all-to-all-start = ((bf16[16,2,8192]{2,1,0:T(2,128)(2,1)}), bf16[16,2,8192]{2,1,0:T(2,128)(2,1)S(1)}, u32[]{:S(2)}, u32[]{:S(2)}) async-start(bf16[16,2,8192]{2,1,0:T(2,128)(2,1)} %reshape.52), calls=%async_computation | async-start | bytes 1048576 | tf_op jit(solution)/shard_map/all_to_all | solution.py:73
  43.3 11.5 reduce.1
  55.8 12.4 all-to-all-done
  68.2 8.7 all-to-all-start.1
  77.6 11.5 reduce.2
  90.0 7.2 all-to-all-done.1
  97.2 6.8 all-to-all-start.2
  107.2 14.1 %all-to-all-done.2 = bf16[16,2,8192]{2,1,0:T(2,128)(2,1)S(1)} async-done(((bf16[16,2,8192]{2,1,0:T(2,128)(2,1)}), bf16[16,2,8192]{2,1,0:T(2,128)(2,1)S(1)}, u32[]{:S(2)}, u32[]{:S(2)}) %all-to-all-start.2) | async-done | bytes 524320 | tf_op jit(solution)/shard_map/all_to_all | solution.py:75
  122.6 50.9 %while.23 = (s32[]{:T(128)}, bf16[4,512,2,64]{1,3,2,0:T(8,128)(2,1)S(1)}, s32[4]{0:T(128)S(1)}, bf16[2048,2,64]{0,2,1:T(8,128)(2,1)}, bf16[2048,2,64]{0,2,1:T(8,...) while((s32[]{:T(128)}, ...), condition=%wide.region_3.4_spmd, body=%wide.region_0.3_spmd.sunk | while | flops 547424256 | bytes 18096304 | solution.py:39
  123.8 6.6 fusion.126
  130.5 4.8 fusion.127
  136.6 6.6 fusion.126
  143.2 4.8 fusion.127
  149.3 6.6 fusion.126
  155.9 4.8 fusion.127
  162.0 6.6 fusion.126
  168.7 4.8 fusion.127
  175.7 11.5 reduce.3
  187.4 20.1 %all_to_all.111 = bf16[16,2,8192]{2,1,0:T(2,128)(2,1)S(1)} all-to-all(bf16[16,2,8192]{2,1,0:T(2,128)(2,1)S(1)} %reshape.58), channel_id=1, replica_groups=mesh['dp'=32,'seq'=16] {'seq'}, dimensions={0} | all-to-all | bytes 1048576 | tf_op jit(solution)/shard_map/all_to_all | solution.py:87
  209.8 228.7 %all-reduce.7.cloned.1.call-done = f32[128,2048]{1,0:T(8,128)} async-done(((f32[128,2048]{1,0:T(8,128)}), f32[128,2048]{1,0:T(8,128)}) %all-reduce.7.cloned.1.call-update) | async-done | bytes 1048592 | tf_op jit(solution)/shard_map/psum | solution.py:89
  443.1 202.7 %all-reduce.9.cloned.1.call-done = f32[128,1408]{1,0:T(8,128)} async-done(((f32[128,1408]{1,0:T(8,128)}), f32[128,1408]{1,0:T(8,128)}) %all-reduce.9.cloned.1.call-update) | async-done | bytes 720912
  647.6 45.7 %all_gather.3 = bf16[128,1408]{1,0:T(8,128)(2,1)S(1)} all-gather(bf16[8,1408]{1,0:T(8,128)(2,1)S(1)} %fusion.70), channel_id=1, replica_groups=mesh['dp'=32,'seq'=16] {'seq'}, dimensions={0}, use_global_device_ids=true | all-gather | bytes 382976 | tf_op jit(solution)/shard_map/all_gather | solution.py:102
  693.9 132.4 %all-reduce.12 = bf16[128,2048]{1,0:T(8,128)(2,1)S(1)} all-reduce(f32[128,2048]{1,0:T(8,128)S(1)} %fusion.88), channel_id=1, replica_groups=mesh['dp'=32,'seq'=16] {'seq'}, use_global_device_ids=true, to_apply=%region_9.10 | all-reduce | flops 262144 | bytes 1572864 | tf_op jit(solution)/shard_map/psum | solution.py:109
  827.4 11.5 reduce.4
  839.9 7.1 all-to-all-start.4
  847.0 18.0 %all-to-all-done.4 = bf16[16,2,8192]{2,1,0:T(2,128)(2,1)S(1)} async-done(((bf16[16,2,8192]{2,1,0:T(2,128)(2,1)}), bf16[16,2,8192]{2,1,0:T(2,128)(2,1)S(1)}, u32[]{:S(2)}, u32[]{:S(2)}) %all-to-all-start.4) | async-done | bytes 524320 | tf_op jit(solution)/shard_map/all_to_all | solution.py:113
  867.0 134.5 %while.24 = (s32[]{:T(128)}, f32[2048,2,64]{0,2,1:T(8,128)S(1)}, bf16[4,512,2,64]{1,3,2,0:T(8,128)(2,1)}, s32[4]{0:T(128)S(1)}, bf16[2048,2,64]{0,2,1:T(8,128)(2...) while((s32[]{:T(128)}, f32[2048,2,64]{0,2,1:T(8,128)S(1)}, ...), condition=%wide.region_14.15_spmd.clone, body=%wide.region_10.14_spmd.clone.sunk | while | flops 1099502592 | bytes 62922960 | solution.py:66
  868.2 6.8 fusion.135
  875.1 6.6 divide_convert_fusion.12
  884.8 4.5 fusion.137
  889.3 11.3 fusion.138
  901.9 6.8 fusion.135
  908.7 6.6 divide_convert_fusion.12
  923.0 11.3 fusion.138
  935.5 6.8 fusion.135
  942.3 6.6 divide_convert_fusion.12
  956.6 11.3 fusion.138
  969.1 6.8 fusion.135
  976.0 6.6 divide_convert_fusion.12
  990.2 11.3 fusion.138
  1005.1 5.0 reshape.50
  1010.1 12.7 reduce.5
  1023.7 6.9 all-to-all-start.5
  1032.8 11.5 reduce.6
  1048.2 10.9 all-to-all-start.6
  1064.8 16.5 %all-to-all-done.6 = bf16[16,2,8192]{2,1,0:T(2,128)(2,1)S(1)} async-done(((bf16[16,2,8192]{2,1,0:T(2,128)(2,1)}), bf16[16,2,8192]{2,1,0:T(2,128)(2,1)S(1)}, u32[]{:S(2)}, u32[]{:S(2)}) %all-to-all-start.6) | async-done | bytes 524320 | tf_op jit(solution)/shard_map/all_to_all | solution.py:120
  1083.2 308.4 %all-reduce.11.cloned.1.call-done = (f32[2048,128]{1,0:T(8,128)}, f32[128,1408]{1,0:T(8,128)}) async-done(((f32[2048,128]{1,0:T(8,128)}, f32[128,1408]{1,0:T(8,128)}), (f32[2048,128]{1,0:T(8,128)}, f32[128,1408]{1,0:T(8,128)})) %all-reduce.11.cloned.1.call-update) | async-done | bytes 1769488 | tf_op jit(solution)/shard_map/psum | solution.py:122
  (105 shorter events, 81.2 us)
Async XLA Ops:
  7.2 431.4 %copy-start = (bf16[2048,128]{1,0:T(8,128)(2,1)S(1)}, bf16[2048,128]{1,0:T(8,128)(2,1)}, u32[]{:S(2)}) copy-start(bf16[2048,128]{1,0:T(8,128)(2,1)} %param.16) | copy-start | bytes 1572868
  7.2 69.7 %copy-start.4 = (bf16[1,128,2048]{2,1,0:T(8,128)(2,1)S(1)}, bf16[1,128,2048]{2,1,0:T(8,128)(2,1)}, u32[]{:S(2)}) copy-start(bf16[1,128,2048]{2,1,0:T(8,128)(2,1)} %param.13) | copy-start | bytes 1572868
  22.6 45.6 %all-to-all-start = ((bf16[16,2,8192]{2,1,0:T(2,128)(2,1)}), bf16[16,2,8192]{2,1,0:T(2,128)(2,1)S(1)}, u32[]{:S(2)}, u32[]{:S(2)}) async-start(bf16[16,2,8192]{2,1,0:T(2,128)(2,1)} %reshape.52), calls=%async_computation | async-start | bytes 1048576 | tf_op jit(solution)/shard_map/all_to_all | solution.py:73
  68.2 29.1 %all-to-all-start.1 = ((bf16[16,2,8192]{2,1,0:T(2,128)(2,1)}), bf16[16,2,8192]{2,1,0:T(2,128)(2,1)S(1)}, u32[]{:S(2)}, u32[]{:S(2)}) async-start(bf16[16,2,8192]{2,1,0:T(2,128)(2,1)} %reshape.54), calls=%async_computation.1 | async-start | bytes 1048576 | tf_op jit(solution)/shard_map/all_to_all | solution.py:74
  97.2 24.1 %all-to-all-start.2 = ((bf16[16,2,8192]{2,1,0:T(2,128)(2,1)}), bf16[16,2,8192]{2,1,0:T(2,128)(2,1)S(1)}, u32[]{:S(2)}, u32[]{:S(2)}) async-start(bf16[16,2,8192]{2,1,0:T(2,128)(2,1)} %reshape.56), calls=%async_computation.2 | async-start | bytes 1048576 | tf_op jit(solution)/shard_map/all_to_all | solution.py:75
  104.0 334.5 %all-reduce.7.cloned.1.call-start = ((), (), s32[]{:S(2)}) async-start(), calls=%async_computation.7 | async-start | bytes 2097152 | tf_op jit(solution)/shard_map/psum | solution.py:89
  173.5 0.8 copy-start.5
  174.3 34.1 %copy-start.9 = (s32[1,128]{1,0:T(1,128)S(1)}, s32[1,128]{1,0:T(1,128)}, u32[]{:S(2)}) copy-start(s32[1,128]{1,0:T(1,128)} %param.14) | copy-start | bytes 1540
  174.3 265.7 %copy-start.6 = (bf16[128,1408]{1,0:T(8,128)(2,1)S(1)}, bf16[128,1408]{1,0:T(8,128)(2,1)}, u32[]{:S(2)}) copy-start(bf16[128,1408]{1,0:T(8,128)(2,1)} %param.17) | copy-start | bytes 1081348
  175.1 470.7 %copy-start.8 = (bf16[1,8,1408]{2,1,0:T(8,128)(2,1)S(1)}, bf16[1,8,1408]{2,1,0:T(8,128)(2,1)}, u32[]{:S(2)}) copy-start(bf16[1,8,1408]{2,1,0:T(8,128)(2,1)} %param.15) | copy-start | bytes 67588
  187.3 506.1 %copy-start.7 = (bf16[128,1408]{1,0:T(8,128)(2,1)S(1)}, bf16[128,1408]{1,0:T(8,128)(2,1)}, u32[]{:S(2)}) copy-start(bf16[128,1408]{1,0:T(8,128)(2,1)} %param.17) | copy-start | bytes 1081348
  209.7 436.0 %all-reduce.9.cloned.1.call-start = ((), (), s32[]{:S(2)}) async-start(), calls=%async_computation.8 | async-start | bytes 1441792
  440.0 253.3 %copy-start.3 = (f32[128,128]{1,0:T(8,128)}, f32[128,128]{1,0:T(8,128)S(1)}, u32[]{:S(2)}) copy-start(f32[128,128]{1,0:T(8,128)S(1)} %fusion.65) | copy-start | bytes 196612
  839.9 25.1 %all-to-all-start.4 = ((bf16[16,2,8192]{2,1,0:T(2,128)(2,1)}), bf16[16,2,8192]{2,1,0:T(2,128)(2,1)S(1)}, u32[]{:S(2)}, u32[]{:S(2)}) async-start(bf16[16,2,8192]{2,1,0:T(2,128)(2,1)} %reshape.60), calls=%async_computation.4 | async-start | bytes 1048576 | tf_op jit(solution)/shard_map/all_to_all | solution.py:113
  867.0 163.7 %copy-start.2 = (f32[128,2048]{1,0:T(8,128)S(1)}, f32[128,2048]{1,0:T(8,128)}, u32[]{:S(2)}) copy-start(f32[128,2048]{1,0:T(8,128)} %all-reduce.7.cloned.1.call-done) | copy-start | bytes 3145732
  1023.7 24.4 %all-to-all-start.5 = ((bf16[16,2,8192]{2,1,0:T(2,128)(2,1)}), bf16[16,2,8192]{2,1,0:T(2,128)(2,1)}, u32[]{:S(2)}, u32[]{:S(2)}) async-start(bf16[16,2,8192]{2,1,0:T(2,128)(2,1)} %reshape.62), calls=%async_computation.5 | async-start | bytes 1048576 | tf_op jit(solution)/shard_map/all_to_all | solution.py:119
  1048.2 33.2 %all-to-all-start.6 = ((bf16[16,2,8192]{2,1,0:T(2,128)(2,1)}), bf16[16,2,8192]{2,1,0:T(2,128)(2,1)S(1)}, u32[]{:S(2)}, u32[]{:S(2)}) async-start(bf16[16,2,8192]{2,1,0:T(2,128)(2,1)} %reshape.64), calls=%async_computation.6 | async-start | bytes 1048576 | tf_op jit(solution)/shard_map/all_to_all | solution.py:120
  1059.1 336.8 %copy-start.1 = (bf16[2048,128]{1,0:T(8,128)(2,1)S(1)}, bf16[2048,128]{1,0:T(8,128)(2,1)}, u32[]{:S(2)}) copy-start(bf16[2048,128]{1,0:T(8,128)(2,1)} %param.16) | copy-start | bytes 1572868
  1059.1 332.5 %all-reduce.11.cloned.1.call-start = ((), (), s32[]{:S(2)}) async-start(), calls=%async_computation.9 | async-start | bytes 3538944 | tf_op jit(solution)/shard_map/psum | solution.py:122
Sparse Core Ops, SparseCore 0:
  209.9 228.6 all-reduce.6
  442.3 203.4 all-reduce.8
  1063.5 328.0 all-reduce.10
where the time goes:
time: 1420 us; the launch traced here: 1400 us
  waiting for transfers between devices  811 us (57%)
  blocking collectives  198 us (14%)
  matrix products  157 us (11%)
  other arithmetic  110 us (8%)
  starting transfers between devices  58.9 us (4%)
  local copies, waits for them, and re-layouts  46.9 us (3%)
  between operations  15.1 us (1%)
    psum x1, waiting for transfers between devices, per_device(): lax.psum((grad_in_local, grad_out_local), 'dp')  308 us
    psum x1, waiting for transfers between devices, per_device(): lax.psum(jnp.dot(selector, token_rows, preferred_element_type=jnp.float32...  229 us
    unnamed x4, waiting for transfers between devices  203 us
    psum x1, blocking collectives, per_device(): grad_pooled = lax.psum(pooled_terms, 'seq').astype(jnp.bfloat16)  132 us
    unnamed x8, other arithmetic  81.8 us
    sub x8, matrix products, block_probs(): weights = jnp.exp(scores - highest)  53.9 us
    all_gather x1, blocking collectives, per_device(): grad_proj = lax.all_gather(grad_rows, 'seq', axis=0, tiled=True)  45.7 us
    dot_general x4, matrix products, step(): jnp.einsum('hqk,khd->qhd', dscore, key_heads, preferred_element_type=jnp....  45.1 us
  transfers between devices with their start and end apart: 9, of which 9 were waited for; matrix products, arithmetic and copies ran while one was open for 4% of the time, Pallas kernels for 0%

commit v1 on v0

v1 whole, which is shorter than its diff:
```python
import functools

import jax
import jax.numpy as jnp
from jax import lax
from jax.experimental import pallas as pl
from jax.experimental.pallas import tpu as pltpu
from jax.sharding import PartitionSpec as P

BF = jnp.bfloat16
F32 = jnp.float32
NS = 16
NY = 4
NZ = 4
TOK = 128
LEN = 2048
FEAT = 128
PATCHES = 128
PY = 32
TEACH = 1408
WIDTH = 2048
GROUP = 16
EPSILON = 1e-06
ROWS = 3 * TOK + 16
BLK = 256
VMEM = 50 * 1024 * 1024

Y_GROUPS = [[y * 4 + z for y in range(4)] for z in range(4)]
Z_GROUPS = [[y * 4 + z for z in range(4)] for y in range(4)]
XC_GROUPS = [[x * 8 + zl * 2 + c for x in range(4) for c in range(2)] for zl in range(4)]
ZL_GROUPS = [[x * 8 + zl * 2 + c for zl in range(4)] for x in range(4) for c in range(2)]

NN = (((1,), (0,)), ((), ()))
NT = (((1,), (1,)), ((), ()))
TN = (((0,), (0,)), ((), ()))


def mm(a, b, dims=NN):
    return lax.dot_general(a, b, dims, preferred_element_type=F32)


def whole(n):
    return [pl.BlockSpec(memory_space=pltpu.VMEM)] * n


def params():
    return pltpu.CompilerParams(vmem_limit_bytes=VMEM)


def sds(shape, dtype):
    return jax.ShapeDtypeStruct(shape, dtype)


def low_half(shape):
    return lax.broadcasted_iota(jnp.int32, shape, 1) < FEAT // 2


def of_head(array, head):
    keep = low_half(array.shape)
    zero = jnp.zeros_like(array)
    return jnp.where(keep, array, zero) if head == 0 else jnp.where(keep, zero, array)


def pack_kernel(q_ref, k_ref, v_ref, ids_ref, out_ref):
    ids = jnp.broadcast_to(ids_ref[...].astype(F32), (16, TOK)).astype(BF)
    for d in range(NS):
        cols = slice(d * FEAT, (d + 1) * FEAT)
        out_ref[d, 0:TOK, :] = q_ref[0, :, cols]
        out_ref[d, TOK:2 * TOK, :] = k_ref[0, :, cols]
        out_ref[d, 2 * TOK:3 * TOK, :] = v_ref[0, :, cols]
        out_ref[d, 3 * TOK:ROWS, :] = ids


def selector(x_ref, block):
    parts = []
    for i in range(BLK // TOK):
        ids = x_ref[block * (BLK // TOK) + i, 3 * TOK:ROWS, :].astype(F32)[0:1, :]
        rows = lax.broadcasted_iota(jnp.int32, (PATCHES, TOK), 0).astype(F32)
        parts.append(jnp.where(rows == ids, 1.0, 0.0).astype(BF))
    return jnp.concatenate(parts, axis=1)


def fwd_kernel(x_ref, p_ref, pp_ref, send_ref, acc_ref):
    block = pl.program_id(0)
    step = BLK // TOK

    @pl.when(block == 0)
    def _():
        acc_ref[...] = jnp.zeros_like(acc_ref)

    keys = x_ref[:, TOK:2 * TOK, :].reshape(LEN, FEAT)
    queries = x_ref[pl.ds(block * step, step), 0:TOK, :].reshape(BLK, FEAT)
    queries = (queries.astype(F32) * 0.125).astype(BF)
    sel = selector(x_ref, block)
    for head in range(2):
        scores = mm(of_head(queries, head), keys, NT)
        highest = jnp.max(scores, axis=1, keepdims=True)
        weights = jnp.exp(scores - highest)
        total = jnp.sum(weights, axis=1, keepdims=True)
        probs = (weights * (1.0 / total)).astype(BF)
        p_ref[head] = probs
        acc_ref[head] += mm(sel, probs)

    @pl.when(block == pl.num_programs(0) - 1)
    def _():
        values = x_ref[:, 2 * TOK:3 * TOK, :].reshape(LEN, FEAT)
        pooled = []
        for head in range(2):
            summed = acc_ref[head].astype(BF)
            pp_ref[head] = summed
            pooled.append(mm(summed, values))
        joined = jnp.where(low_half((PATCHES, FEAT)), pooled[0], pooled[1])
        joined = (joined * (1.0 / GROUP)).astype(BF)
        for d in range(NS):
            y = d // NZ
            send_ref[d] = joined[y * PY:(y + 1) * PY, :]


def proj1_kernel(r_ref, win_ref, wout_ref, teacher_ref, pooled_ref, preact_ref, hidden_ref, send_ref):
    for s in range(NS):
        pooled_ref[:, s * FEAT:(s + 1) * FEAT] = r_ref[s]
    pooled = pooled_ref[...]
    partial = None
    for y in range(NY):
        cols = slice(y * FEAT, (y + 1) * FEAT)
        preact = mm(pooled, win_ref[y])
        hidden = (preact * jax.nn.sigmoid(preact)).astype(BF)
        preact_ref[:, cols] = preact
        hidden_ref[:, cols] = hidden
        term = mm(hidden, wout_ref[y])
        partial = term if partial is None else partial + term
    send_ref[0:PY, :] = partial.astype(BF)
    own = teacher_ref[0]
    send_ref[PY:PY + 16, :] = jnp.concatenate([own, own], axis=0)


def proj2_kernel(r_ref, preact_ref, hidden_ref, pooled_ref, win_ref, wout_ref, back_ref, side_ref):
    proj = r_ref[0, 0:PY, :].astype(F32)
    for z in range(1, NZ):
        proj = proj + r_ref[z, 0:PY, :].astype(F32)
    target = jnp.concatenate(
        [r_ref[z, PY:PY + 16, :].astype(F32)[0:8, :] for z in range(NZ)], axis=0
    )
    scale = 1.0 / TEACH
    cross = jnp.sum(proj * target, axis=1, keepdims=True) * scale
    proj_power = jnp.sum(proj * proj, axis=1, keepdims=True) * scale + EPSILON
    teach_power = jnp.sum(target * target, axis=1, keepdims=True) * scale + EPSILON
    grad = (-(target - cross / proj_power * proj) / jnp.sqrt(proj_power * teach_power)).astype(BF)
    pooled = pooled_ref[...]
    terms = None
    for y in range(NY):
        cols = slice(y * FEAT, (y + 1) * FEAT)
        grad_hidden = mm(grad, wout_ref[y], NT)
        preact = preact_ref[:, cols]
        sigma = jax.nn.sigmoid(preact)
        grad_pre = (grad_hidden * sigma * (1.0 + preact * (1.0 - sigma))).astype(BF)
        term = mm(grad_pre, win_ref[y], NT)
        terms = term if terms is None else terms + term
        side_ref[y, :, 0:WIDTH] = pooled
        side_ref[y, :, WIDTH:WIDTH + TEACH] = grad
        side_ref[y, :, WIDTH + TEACH:WIDTH + TEACH + FEAT] = hidden_ref[:, cols]
        side_ref[y, :, WIDTH + TEACH + FEAT:WIDTH + TEACH + 2 * FEAT] = grad_pre
    terms = terms.astype(BF)
    for d in range(NS):
        back_ref[d] = terms[:, d * FEAT:(d + 1) * FEAT]


def bwd_kernel(r_ref, x_ref, pp_ref, p_ref, out_ref, g_ref):
    block = pl.program_id(0)
    step = BLK // TOK

    @pl.when(block == 0)
    def _():
        for y in range(NY):
            summed = r_ref[y * NZ].astype(F32)
            for z in range(1, NZ):
                summed = summed + r_ref[y * NZ + z].astype(F32)
            rounded = summed.astype(BF).astype(F32) * (1.0 / GROUP)
            g_ref[y * PY:(y + 1) * PY, :] = rounded.astype(BF)
        grad = g_ref[...]
        parts = [mm(pp_ref[head], grad, TN) for head in range(2)]
        values_grad = jnp.where(low_half((LEN, FEAT)), parts[0], parts[1]).astype(BF)
        out_ref[:, TOK:2 * TOK, :] = values_grad.reshape(NS, TOK, FEAT)

    keys = x_ref[:, TOK:2 * TOK, :].reshape(LEN, FEAT)
    values = x_ref[:, 2 * TOK:3 * TOK, :].reshape(LEN, FEAT)
    sel = selector(x_ref, block)
    upstream = (mm(sel, g_ref[...], TN) * 0.125).astype(BF)
    parts = []
    for head in range(2):
        dprob = mm(of_head(upstream, head), values, NT)
        probs = p_ref[head].astype(F32)
        delta = jnp.sum(probs * dprob, axis=1, keepdims=True)
        dscore = (probs * (dprob - delta)).astype(BF)
        parts.append(mm(dscore, keys))
    rows = jnp.where(low_half((BLK, FEAT)), parts[0], parts[1]).astype(BF)
    out_ref[pl.ds(block * step, step), 0:TOK, :] = rows.reshape(step, TOK, FEAT)


def weights_kernel(r_ref, out_ref):
    full = [r_ref[y] for y in range(NY)]
    joined = jnp.concatenate(full, axis=0)
    hidden = joined[:, WIDTH + TEACH:WIDTH + TEACH + FEAT]
    grad_pre = joined[:, WIDTH + TEACH + FEAT:WIDTH + TEACH + 2 * FEAT]
    out_ref[0:WIDTH, :] = mm(joined[:, 0:WIDTH], grad_pre, TN).astype(BF)
    grad_out = mm(hidden, joined[:, WIDTH:WIDTH + TEACH], TN).astype(BF)
    for c in range(TEACH // FEAT):
        out_ref[WIDTH + c * FEAT:WIDTH + (c + 1) * FEAT, :] = grad_out[:, c * FEAT:(c + 1) * FEAT]


def unpack_kernel(r_ref, dq_ref, dv_ref):
    for s in range(NS):
        cols = slice(s * FEAT, (s + 1) * FEAT)
        dq_ref[0, :, cols] = r_ref[s, 0:TOK, :]
        dv_ref[0, :, cols] = r_ref[s, TOK:2 * TOK, :]


def exchange(array, axis, groups=None):
    return lax.all_to_all(array, axis, 0, 0, axis_index_groups=groups, tiled=True)


def gather(array, axis, groups=None):
    return lax.all_gather(array, axis, axis=0, axis_index_groups=groups, tiled=False)


def per_device(query, key, value, patch_map, teacher, proj_in, proj_out):
    win = gather(proj_in, "seq", Y_GROUPS)
    wout = gather(proj_out, "seq", Y_GROUPS)

    packed = pl.pallas_call(
        pack_kernel,
        out_shape=sds((NS, ROWS, FEAT), BF),
        in_specs=whole(4),
        out_specs=whole(1)[0],
        compiler_params=params(),
    )(query, key, value, patch_map)
    x = exchange(packed, "seq")

    steps = LEN // BLK
    probs, pooled_probs, pooled_out = pl.pallas_call(
        fwd_kernel,
        grid=(steps,),
        out_shape=(
            sds((2, LEN, LEN), BF),
            sds((2, PATCHES, LEN), BF),
            sds((NS, PY, FEAT), BF),
        ),
        in_specs=[pl.BlockSpec((NS, ROWS, FEAT), lambda i: (0, 0, 0))],
        out_specs=(
            pl.BlockSpec((2, BLK, LEN), lambda i: (0, i, 0)),
            pl.BlockSpec((2, PATCHES, LEN), lambda i: (0, 0, 0)),
            pl.BlockSpec((NS, PY, FEAT), lambda i: (0, 0, 0)),
        ),
        scratch_shapes=[pltpu.VMEM((2, PATCHES, LEN), F32)],
        compiler_params=params(),
    )(x)
    pooled_in = exchange(pooled_out, "seq")

    pooled, preact, hidden, partial = pl.pallas_call(
        proj1_kernel,
        out_shape=(
            sds((PY, WIDTH), BF),
            sds((PY, NY * FEAT), F32),
            sds((PY, NY * FEAT), BF),
            sds((PY + 16, TEACH), BF),
        ),
        in_specs=whole(4),
        out_specs=tuple(whole(4)),
        compiler_params=params(),
    )(pooled_in, win, wout, teacher)
    partials = gather(partial, "seq", Z_GROUPS)

    back, side = pl.pallas_call(
        proj2_kernel,
        out_shape=(
            sds((NS, PY, FEAT), BF),
            sds((NY, PY, WIDTH + TEACH + 2 * FEAT), BF),
        ),
        in_specs=whole(6),
        out_specs=tuple(whole(2)),
        compiler_params=params(),
    )(partials, preact, hidden, pooled, win, wout)
    back_in = exchange(back, "seq")
    side_in = exchange(side, "seq", Y_GROUPS)

    grads = pl.pallas_call(
        bwd_kernel,
        grid=(steps,),
        out_shape=sds((NS, 2 * TOK, FEAT), BF),
        in_specs=[
            pl.BlockSpec((NS, PY, FEAT), lambda i: (0, 0, 0)),
            pl.BlockSpec((NS, ROWS, FEAT), lambda i: (0, 0, 0)),
            pl.BlockSpec((2, PATCHES, LEN), lambda i: (0, 0, 0)),
            pl.BlockSpec((2, BLK, LEN), lambda i: (0, i, 0)),
        ],
        out_specs=pl.BlockSpec((NS, 2 * TOK, FEAT), lambda i: (0, 0, 0)),
        scratch_shapes=[pltpu.VMEM((PATCHES, FEAT), BF)],
        compiler_params=params(),
    )(back_in, x, pooled_probs, probs)
    grads_in = exchange(grads, "seq")

    terms = pl.pallas_call(
        weights_kernel,
        out_shape=sds((WIDTH + TEACH, FEAT), BF),
        in_specs=whole(1),
        out_specs=whole(1)[0],
        compiler_params=params(),
    )(side_in)
    rows = WIDTH + TEACH
    part = exchange(terms.reshape(8, rows // 8, FEAT), "dp", XC_GROUPS)
    part = jnp.sum(part.astype(F32), axis=0).astype(BF)
    part = exchange(part.reshape(4, rows // 32, FEAT), "dp", ZL_GROUPS)
    part = jnp.sum(part.astype(F32), axis=0).astype(BF)
    part = gather(part, "dp", ZL_GROUPS).reshape(rows // 8, FEAT)
    total = gather(part, "dp", XC_GROUPS).reshape(rows, FEAT).astype(F32)
    grad_in = total[:WIDTH]
    grad_out = total[WIDTH:].reshape(TEACH // FEAT, FEAT, FEAT).transpose(1, 0, 2).reshape(FEAT, TEACH)

    grad_query, grad_value = pl.pallas_call(
        unpack_kernel,
        out_shape=(sds((1, TOK, WIDTH), BF), sds((1, TOK, WIDTH), BF)),
        in_specs=whole(1),
        out_specs=tuple(whole(2)),
        compiler_params=params(),
    )(grads_in)
    return (grad_query, grad_value, grad_in, grad_out)


def solution(mesh):
    placed = (
        P("dp", "seq", None),
        P("dp", "seq", None),
        P("dp", "seq", None),
        P("dp", "seq"),
        P("dp", "seq", None),
        P(None, "seq"),
        P("seq", None),
    )
    return jax.shard_map(
        per_device,
        mesh=mesh,
        in_specs=placed,
        out_specs=(P("dp", "seq", None), P("dp", "seq", None), P(None, "seq"), P("seq", None)),
        check_vma=False,
    )
```

time: 1420 us -> 348 us (0.25); the launches traced: 1400 us -> 347 us
  waiting for transfers between devices: 811 us -> 106 us
  matrix products: 157 us -> 0 us
  other arithmetic: 110 us -> 1.31 us
  blocking collectives: 198 us -> 127 us
  Pallas kernels: 0 us -> 46.1 us
  local copies, waits for them, and re-layouts: 46.9 us -> 9.91 us
  starting transfers between devices: 58.9 us -> 42.9 us
    psum x2 -> x0, waiting for transfers between devices: 537 us -> none  [the longest x1 308 us: per_device(): lax.psum((grad_in_local, grad_out_local), 'dp')]
    unnamed x4 -> x2, waiting for transfers between devices: 203 us -> 1.38 us
    psum x1 -> x0, blocking collectives: 132 us -> none  [per_device(): grad_pooled = lax.psum(pooled_terms, 'seq').astype(jnp.bfloat16)]
    dot_general x24 -> x0, matrix products: 103 us -> none  [the longest x4 45.1 us: step(): jnp.einsum('hqk,khd->qhd', dscore, key_heads, preferred_element_type=jnp....]
    unnamed x8 -> x0, other arithmetic: 81.8 us -> none
    sub x8 -> x0, matrix products: 53.9 us -> none  [block_probs(): weights = jnp.exp(scores - highest)]
    pallas_call x0 -> x7, Pallas kernels: none -> 46.1 us  [the longest x1 19.7 us: per_device(): pl.pallas_call(fwd_kernel, grid=(steps,), out_shape=(sds((2, LEN, LEN), B...]
    all_gather x1 -> x3, blocking collectives: 45.7 us -> 89.3 us  [gather(): lax.all_gather(array, axis, axis=0, axis_index_groups=groups, tiled=False)]
  transfers between devices with their start and end apart: 9 -> 7, of which waited for: 9 -> 3; matrix products, arithmetic and copies ran while one was open for 4% -> 1% of each run, Pallas kernels for 0% -> 11%
where the time goes in v1:
time: 348 us; the launch traced here: 347 us
  blocking collectives  127 us (36%)
  waiting for transfers between devices  106 us (30%)
  Pallas kernels  46.1 us (13%)
  starting transfers between devices  42.9 us (12%)
  between operations  14.1 us (4%)
  local copies, waits for them, and re-layouts  9.91 us (3%)
    all_to_all x5, waiting for transfers between devices, exchange(): lax.all_to_all(array, axis, 0, 0, axis_index_groups=groups, tiled=True)  105 us
    all_gather x3, blocking collectives, gather(): lax.all_gather(array, axis, axis=0, axis_index_groups=groups, tiled=False)  89.3 us
    all_to_all x5, starting transfers between devices, exchange(): lax.all_to_all(array, axis, 0, 0, axis_index_groups=groups, tiled=True)  42.9 us
    all_to_all x2, blocking collectives, exchange(): lax.all_to_all(array, axis, 0, 0, axis_index_groups=groups, tiled=True)  37.7 us
    pallas_call x1, Pallas kernels, per_device(): pl.pallas_call(fwd_kernel, grid=(steps,), out_shape=(sds((2, LEN, LEN), B...  19.7 us
    pallas_call x1, Pallas kernels, per_device(): pl.pallas_call(bwd_kernel, grid=(steps,), out_shape=sds((NS, 2 * TOK, FEA...  18.2 us
    unnamed x18, local copies, waits for them, and re-layouts  7.89 us
  transfers between devices with their start and end apart: 7, of which 3 were waited for; matrix products, arithmetic and copies ran while one was open for 1% of the time, Pallas kernels for 11%

profile of v1, /device:TPU:1, one launch (start us, length us, event | category | flops | bytes accessed | tf_op | source)
XLA Modules:
  0.0 347.4 jit_solution(8781030789509203754)
XLA Ops:
  7.2 0.0 copy-start.3
  7.2 1.0 copy-done.3
  8.2 0.0 copy-start.4
  8.2 1.0 copy-done.4
  9.3 0.0 copy-start.5
  9.3 1.0 copy-done.5
  10.3 0.0 copy-start.7
  10.3 0.7 copy-done.7
  10.9 1.5 shard_map.102
  12.4 18.4 %all-to-all-start = ((bf16[16,400,128]{2,1,0:T(8,128)(2,1)}), bf16[16,400,128]{2,1,0:T(8,128)(2,1)S(1)}, u32[]{:S(2)}, u32[]{:S(2)}) async-start(bf16[16,400,128]{2,1,0:T(8,128)(2,1)} %shard_map.102), calls=%async_computation | async-start | bytes 3276800 | tf_op jit(solution)/shard_map/all_to_all | solution.py:219
  30.8 0.0 copy-start.6
  30.8 0.0 all-gather.11.cloned.1.call-start
  30.9 0.7 all-gather.11.cloned.1.call-update
  31.6 0.0 all-gather.9.cloned.1.call-start
  31.6 0.7 all-gather.9.cloned.1.call-update
  32.3 74.9 %all-to-all-done.x_ref = bf16[16,400,128]{2,1,0:T(8,128)(2,1)S(1)} async-done(((bf16[16,400,128]{2,1,0:T(8,128)(2,1)}), bf16[16,400,128]{2,1,0:T(8,128)(2,1)S(1)}, u32[]{:S(2)}, u32[]{:S(2)}) %all-to-all-start) | async-done | bytes 1638432 | tf_op jit(solution)/shard_map/all_to_all | solution.py:219
  107.2 19.7 %shard_map.103 = (bf16[2,2048,2048]{2,1,0:T(8,128)(2,1)}, bf16[2,128,2048]{2,1,0:T(8,128)(2,1)S(1)}, bf16[16,32,128]{2,1,0:T(8,128)(2,1)}) custom-call(bf16[16,400,128]{2,1,0:T(8,128)(2,1)S(1)} %all-to-all-done.x_ref), custom_call_target="tpu_custom_call" | custom-call | tf_op jit(solution)/shard_map/pallas_call | solution.py:240
  126.9 9.4 %all-to-all-start.1 = ((bf16[16,32,128]{2,1,0:T(8,128)(2,1)}), bf16[16,32,128]{2,1,0:T(8,128)(2,1)S(1)}, u32[]{:S(2)}, u32[]{:S(2)}) async-start(bf16[16,32,128]{2,1,0:T(8,128)(2,1)} %get-tuple-element.15), calls=%async_computation.1 | async-start | bytes 262144 | tf_op jit(solution)/shard_map/all_to_all | solution.py:219
  136.3 0.0 all-gather.11.cloned.1.call-done
  136.4 0.0 all-gather.9.cloned.1.call-done
  136.4 15.9 %all-to-all-done.1.r_ref = bf16[16,32,128]{2,1,0:T(8,128)(2,1)S(1)} async-done(((bf16[16,32,128]{2,1,0:T(8,128)(2,1)}), bf16[16,32,128]{2,1,0:T(8,128)(2,1)S(1)}, u32[]{:S(2)}, u32[]{:S(2)}) %all-to-all-start.1) | async-done | bytes 131104 | tf_op jit(solution)/shard_map/all_to_all | solution.py:219
  152.3 0.0 copy-done.6
  152.3 0.0 copy-start
  152.3 1.6 copy-done
  153.9 0.0 copy-start.1
  153.9 1.4 copy-done.1
  155.3 1.0 shard_map.104
  156.3 19.6 %all-gather.2 = bf16[192,1408]{1,0:T(8,128)(2,1)S(1)} all-gather(bf16[48,1408]{1,0:T(8,128)(2,1)S(1)} %get-tuple-element.16), channel_id=4, replica_groups={{0,1,2,3},{4,5,6,7},{8,9,10,11},{12,13,14,15},{16,17,18,19},{20,21,22,2..., dimensions={0}, use_global_device_ids=true | all-gather | bytes 675840 | tf_op jit(solution)/shard_map/all_gather | solution.py:223
  175.9 0.0 copy-done.2
  175.9 4.0 %shard_map.105 = (bf16[16,32,128]{2,1,0:T(8,128)(2,1)}, bf16[4,32,3712]{2,1,0:T(8,128)(2,1)S(1)}) custom-call(bf16[4,48,1408]{2,1,0:T(8,128)(2,1)S(1)} %bitcast.14, f32[32,512]{1,0:T(8,128)S(1)} %get-tuple-element.17.preact_ref, bf16[32,512]{1,0:T(8,128)(2,1)S(1)} %get-tuple-element.18.hidden_ref, bf16[32,2048]{1,0:T(8,128)(2,1)S(1)} %get-tuple-element.19.pooled_ref, ...), custom_call_target="tpu_custom_call" | custom-call | tf_op jit(solution)/shard_map/pallas_call | solution.py:273
  179.9 13.0 %all_to_all.35.r_ref = bf16[4,32,3712]{2,1,0:T(8,128)(2,1)S(1)} all-to-all(bf16[4,32,3712]{2,1,0:T(8,128)(2,1)S(1)} %get-tuple-element.25), channel_id=1, replica_groups={{0,4,8,12},{1,5,9,13},{2,6,10,14},{3,7,11,15},{16,20,24,28},{17,21,25,2..., dimensions={0} | all-to-all | bytes 1900544 | tf_op jit(solution)/shard_map/all_to_all | solution.py:219
  192.9 0.4 shard_map.108
  193.4 24.7 %all_to_all.36 = bf16[8,432,128]{2,1,0:T(8,128)(2,1)} all-to-all(bf16[8,432,128]{2,1,0:T(8,128)(2,1)S(1)} %bitcast.13), channel_id=1, replica_groups={{0,16,128,144,256,272,384,400},{32,48,160,176,288,304,416,432},{64,80,1..., dimensions={0} | all-to-all | bytes 1769472 | tf_op jit(solution)/shard_map/all_to_all | solution.py:219
  218.0 7.1 %all-to-all-start.2 = ((bf16[16,32,128]{2,1,0:T(8,128)(2,1)}), bf16[16,32,128]{2,1,0:T(8,128)(2,1)S(1)}, u32[]{:S(2)}, u32[]{:S(2)}) async-start(bf16[16,32,128]{2,1,0:T(8,128)(2,1)} %get-tuple-element.20), calls=%async_computation.2 | async-start | bytes 262144 | tf_op jit(solution)/shard_map/all_to_all | solution.py:219
  225.1 1.3 reduce_sum.24
  226.4 0.7 reshape.24
  227.1 13.8 %all-to-all-done.2.r_ref = bf16[16,32,128]{2,1,0:T(8,128)(2,1)S(1)} async-done(((bf16[16,32,128]{2,1,0:T(8,128)(2,1)}), bf16[16,32,128]{2,1,0:T(8,128)(2,1)S(1)}, u32[]{:S(2)}, u32[]{:S(2)}) %all-to-all-start.2) | async-done | bytes 131104 | tf_op jit(solution)/shard_map/all_to_all | solution.py:219
  240.9 4.4 %all-to-all-start.6 = ((bf16[4,108,128]{2,1,0:T(8,128)(2,1)}), bf16[4,108,128]{2,1,0:T(8,128)(2,1)S(1)}, u32[]{:S(2)}, u32[]{:S(2)}) async-start(bf16[4,108,128]{2,1,0:T(8,128)(2,1)} %reshape.24), calls=%async_computation.6 | async-start | bytes 229376 | tf_op jit(solution)/shard_map/all_to_all | solution.py:219
  245.3 18.2 %shard_map.106 = bf16[16,256,128]{2,1,0:T(8,128)(2,1)} custom-call(bf16[16,32,128]{2,1,0:T(8,128)(2,1)S(1)} %all-to-all-done.2.r_ref, bf16[16,400,128]{2,1,0:T(8,128)(2,1)S(1)} %all-to-all-done.x_ref, bf16[2,128,2048]{2,1,0:T(8,128)(2,1)S(1)} %get-tuple-element.21.pp_ref, bf16[2,2048,2048]{2,1,0:T(8,128)(2,1)} %get-tuple-element.22.p_ref), custom_call_target="tpu_custom_call" | custom-call | tf_op jit(solution)/shard_map/pallas_call | solution.py:286
  263.5 0.0 all-to-all-done.6
  263.5 3.7 %all-to-all-start.3 = ((bf16[16,256,128]{2,1,0:T(8,128)(2,1)}), bf16[16,256,128]{2,1,0:T(8,128)(2,1)S(1)}, u32[]{:S(2)}, u32[]{:S(2)}) async-start(bf16[16,256,128]{2,1,0:T(8,128)(2,1)} %shard_map.106), calls=%async_computation.3 | async-start | bytes 2097152 | tf_op jit(solution)/shard_map/all_to_all | solution.py:219
  267.2 54.8 %all-gather.5 = bf16[4,108,128]{2,1,0:T(8,128)(2,1)S(1)} all-gather(bf16[1,108,128]{2,1,0:T(8,128)(2,1)S(1)} %bitcast.17), channel_id=5, replica_groups={{0,32,64,96},{16,48,80,112},{128,160,192,224},{144,176,208,240},{256,28..., dimensions={0}, use_global_device_ids=true | all-gather | bytes 138240 | tf_op jit(solution)/shard_map/all_gather | solution.py:223
  321.9 14.9 %all-gather.4 = bf16[3456,128]{1,0:T(8,128)(2,1)S(1)} all-gather(bf16[432,128]{1,0:T(8,128)(2,1)S(1)} %reshape.38), channel_id=6, replica_groups={{0,16,128,144,256,272,384,400},{32,48,160,176,288,304,416,432},{64,80,1..., dimensions={0}, use_global_device_ids=true | all-gather | bytes 995328 | tf_op jit(solution)/shard_map/all_gather | solution.py:223
  336.9 1.0 slice.9
  337.9 0.3 copy.14
  338.2 1.1 copy.15
  339.3 0.0 all-to-all-done.3.r_ref
  339.3 1.3 shard_map.107
  (4 shorter events, 0.1 us)
Async XLA Ops:
  7.2 1.0 copy-start.3
  8.2 1.0 copy-start.4
  9.3 1.0 copy-start.5
  10.3 0.7 copy-start.7
  12.4 94.8 %all-to-all-start = ((bf16[16,400,128]{2,1,0:T(8,128)(2,1)}), bf16[16,400,128]{2,1,0:T(8,128)(2,1)S(1)}, u32[]{:S(2)}, u32[]{:S(2)}) async-start(bf16[16,400,128]{2,1,0:T(8,128)(2,1)} %shard_map.102), calls=%async_computation | async-start | bytes 3276800 | tf_op jit(solution)/shard_map/all_to_all | solution.py:219
  30.8 121.5 %copy-start.6 = (bf16[1,8,1408]{2,1,0:T(8,128)(2,1)S(1)}, bf16[1,8,1408]{2,1,0:T(8,128)(2,1)}, u32[]{:S(2)}) copy-start(bf16[1,8,1408]{2,1,0:T(8,128)(2,1)} %teacher_ref.1) | copy-start | bytes 67588
  30.8 105.5 %all-gather.11.cloned.1.call-start = ((), (), s32[]{:S(2)}) async-start(), calls=%async_computation.8 | async-start | bytes 1802240 | tf_op jit(solution)/shard_map/all_gather | solution.py:223
  31.6 104.8 %all-gather.9.cloned.1.call-start = ((), (), s32[]{:S(2)}) async-start(), calls=%async_computation.7 | async-start | bytes 2621440 | tf_op jit(solution)/shard_map/all_gather | solution.py:223
  126.9 25.4 %all-to-all-start.1 = ((bf16[16,32,128]{2,1,0:T(8,128)(2,1)}), bf16[16,32,128]{2,1,0:T(8,128)(2,1)S(1)}, u32[]{:S(2)}, u32[]{:S(2)}) async-start(bf16[16,32,128]{2,1,0:T(8,128)(2,1)} %get-tuple-element.15), calls=%async_computation.1 | async-start | bytes 262144 | tf_op jit(solution)/shard_map/all_to_all | solution.py:219
  152.3 1.6 copy-start
  153.9 1.4 copy-start.1
  155.3 20.6 %copy-start.2 = (bf16[512,1408]{1,0:T(8,128)(2,1)S(1)}, bf16[512,1408]{1,0:T(8,128)(2,1)}, u32[]{:S(2)}) copy-start(bf16[512,1408]{1,0:T(8,128)(2,1)} %all-gather.11.cloned.1.call-done) | copy-start | bytes 4325380
  218.0 22.9 %all-to-all-start.2 = ((bf16[16,32,128]{2,1,0:T(8,128)(2,1)}), bf16[16,32,128]{2,1,0:T(8,128)(2,1)S(1)}, u32[]{:S(2)}, u32[]{:S(2)}) async-start(bf16[16,32,128]{2,1,0:T(8,128)(2,1)} %get-tuple-element.20), calls=%async_computation.2 | async-start | bytes 262144 | tf_op jit(solution)/shard_map/all_to_all | solution.py:219
  240.9 22.6 %all-to-all-start.6 = ((bf16[4,108,128]{2,1,0:T(8,128)(2,1)}), bf16[4,108,128]{2,1,0:T(8,128)(2,1)S(1)}, u32[]{:S(2)}, u32[]{:S(2)}) async-start(bf16[4,108,128]{2,1,0:T(8,128)(2,1)} %reshape.24), calls=%async_computation.6 | async-start | bytes 229376 | tf_op jit(solution)/shard_map/all_to_all | solution.py:219
  263.5 75.8 %all-to-all-start.3 = ((bf16[16,256,128]{2,1,0:T(8,128)(2,1)}), bf16[16,256,128]{2,1,0:T(8,128)(2,1)S(1)}, u32[]{:S(2)}, u32[]{:S(2)}) async-start(bf16[16,256,128]{2,1,0:T(8,128)(2,1)} %shard_map.106), calls=%async_computation.3 | async-start | bytes 2097152 | tf_op jit(solution)/shard_map/all_to_all | solution.py:219
Sparse Core Ops, SparseCore 0:
  33.8 39.3 all-gather.10
  75.3 39.2 all-gather.8

commit v2 on v1

v2 whole, which is shorter than its diff:
```python
import functools

import jax
import jax.numpy as jnp
from jax import lax
from jax.experimental import pallas as pl
from jax.experimental.pallas import tpu as pltpu
from jax.sharding import PartitionSpec as P

BF = jnp.bfloat16
F32 = jnp.float32
NS = 16
NY = 4
NZ = 4
TOK = 128
LEN = 2048
FEAT = 128
PATCHES = 128
PY = 32
TEACH = 1408
WIDTH = 2048
GROUP = 16
EPSILON = 1e-06
ROWS = 2 * TOK + 16
TROWS = 96
EARLY = 4224
LATE = 1408 + 512
ROWS_DP = (2048 + 1408) // 8
FBLK = 512
BBLK = 256
CHUNK = 16
PARTS = 4
MIB = 1024 * 1024

Y_GROUPS = [[y * 4 + z for y in range(4)] for z in range(4)]
Z_GROUPS = [[y * 4 + z for z in range(4)] for y in range(4)]
Y_SHIFT = [[(y * 4 + z, (y + k) % 4 * 4 + z) for y in range(4) for z in range(4)] for k in range(4)]
Z_SHIFT = [[(y * 4 + z, y * 4 + (z + k) % 4) for y in range(4) for z in range(4)] for k in range(4)]
XC_GROUPS = [[x * 8 + zl * 2 + c for x in range(4) for c in range(2)] for zl in range(4)]
ZL_GROUPS = [[x * 8 + zl * 2 + c for zl in range(4)] for x in range(4) for c in range(2)]

NN = (((1,), (0,)), ((), ()))
NT = (((1,), (1,)), ((), ()))
TN = (((0,), (0,)), ((), ()))


def mm(a, b, dims=NN):
    return lax.dot_general(a, b, dims, preferred_element_type=F32)


def whole(n):
    return [pl.BlockSpec(memory_space=pltpu.VMEM)] * n


def params(mib=12):
    return pltpu.CompilerParams(vmem_limit_bytes=mib * MIB)


def sds(shape, dtype):
    return jax.ShapeDtypeStruct(shape, dtype)


def low_half(shape):
    return lax.broadcasted_iota(jnp.int32, shape, 1) < FEAT // 2


def of_head(array, head):
    keep = low_half(array.shape)
    zero = jnp.zeros_like(array)
    return jnp.where(keep, array, zero) if head == 0 else jnp.where(keep, zero, array)


def pack_kernel(q_ref, k_ref, ids_ref, out_ref):
    ids = jnp.broadcast_to(ids_ref[...].astype(F32), (16, TOK)).astype(BF)
    for i in range(NS // PARTS):
        cols = slice(i * FEAT, (i + 1) * FEAT)
        out_ref[i, 0:TOK, :] = q_ref[0, :, cols]
        out_ref[i, TOK:2 * TOK, :] = k_ref[0, :, cols]
        out_ref[i, 2 * TOK:ROWS, :] = ids


def split_value_kernel(v_ref, *out_refs):
    y = lax.axis_index("seq") // NZ
    for k in range(NY):
        for z in range(NZ):
            at = pl.multiple_of((y + k) % NY * (NZ * FEAT) + z * FEAT, FEAT)
            out_refs[k][z] = v_ref[0, :, pl.ds(at, FEAT)]


def turn_value_kernel(a_ref, b_ref, c_ref, d_ref, teacher_ref, *out_refs):
    z = lax.axis_index("seq") % NZ
    own = teacher_ref[0].astype(F32)
    for k in range(NZ):
        for c in range(0, TROWS // 8, 2):
            first = own[:, c * FEAT:(c + 1) * FEAT]
            second = own[:, (c + 1) * FEAT:(c + 2) * FEAT] if (c + 1) * FEAT < TEACH else first
            out_refs[k][c * 8:c * 8 + 16, :] = jnp.concatenate([first, second], axis=0).astype(BF)
        for i, ref in enumerate((a_ref, b_ref, c_ref, d_ref)):
            rows = slice(TROWS + i * TOK, TROWS + (i + 1) * TOK)
            out_refs[k][rows, :] = ref[(z + k) % NZ]


def selector(x_ref, first, count):
    parts = []
    for i in range(count):
        ids = x_ref[first + i, 2 * TOK:ROWS, :].astype(F32)[0:1, :]
        rows = lax.broadcasted_iota(jnp.int32, (PATCHES, TOK), 0).astype(F32)
        parts.append(jnp.where(rows == ids, 1.0, 0.0).astype(BF))
    return jnp.concatenate(parts, axis=1)


def fwd_kernel(x_ref, p_ref, pp_ref, acc_ref, s0_ref, s1_ref):
    block = pl.program_id(0)
    step = FBLK // TOK

    @pl.when(block == 0)
    def _():
        acc_ref[...] = jnp.zeros_like(acc_ref)

    keys = x_ref[:, TOK:2 * TOK, :].reshape(LEN, FEAT)
    queries = x_ref[pl.ds(block * step, step), 0:TOK, :].reshape(FBLK, FEAT)
    queries = (queries.astype(F32) * 0.125).astype(BF)
    sel = selector(x_ref, block * step, step)
    score_refs = (s0_ref, s1_ref)
    for head in range(2):
        score_refs[head][...] = mm(of_head(queries, head), keys, NT)
    for head in range(2):
        for c in range(0, FBLK, CHUNK):
            scores = score_refs[head][c:c + CHUNK, :]
            weights = jnp.exp(scores - jnp.max(scores, axis=1, keepdims=True))
            total = jnp.sum(weights, axis=1, keepdims=True)
            p_ref[head, c:c + CHUNK, :] = (weights * (1.0 / total)).astype(BF)
        acc_ref[head] += mm(sel, p_ref[head])

    @pl.when(block == pl.num_programs(0) - 1)
    def _():
        for head in range(2):
            pp_ref[head] = acc_ref[head].astype(BF)


def pool_kernel(pp_ref, a_ref, b_ref, c_ref, d_ref, send_ref, v_ref, target_ref):
    y = lax.axis_index("seq") // NZ
    z = lax.axis_index("seq") % NZ
    for k, ref in enumerate((a_ref, b_ref, c_ref, d_ref)):
        source = (z + NZ - k) % NZ
        for i in range(NY):
            v_ref[(y + NY - i) % NY * NZ + source] = ref[TROWS + i * TOK:TROWS + (i + 1) * TOK, :]
        at = pl.ds(pl.multiple_of(source * 8, 8), 8)
        for c in range(0, TROWS // 8, 2):
            pair = ref[c * 8:c * 8 + 16, :].astype(F32)
            target_ref[at, c * FEAT:(c + 1) * FEAT] = pair[0:8, :]
            if (c + 1) * FEAT < TEACH:
                target_ref[at, (c + 1) * FEAT:(c + 2) * FEAT] = pair[8:16, :]
    values = v_ref[...].reshape(LEN, FEAT)
    pooled = [mm(pp_ref[head], values) for head in range(2)]
    joined = jnp.where(low_half((PATCHES, FEAT)), pooled[0], pooled[1])
    joined = (joined * (1.0 / GROUP)).astype(BF)
    for d in range(NS):
        send_ref[d] = joined[d // NZ * PY:(d // NZ + 1) * PY, :]


def proj1_kernel(r_ref, win_ref, wout_ref, early_ref, preact_ref, send_ref, acc_ref):
    y = pl.program_id(0)

    @pl.when(y == 0)
    def _():
        for s in range(NS):
            early_ref[:, s * FEAT:(s + 1) * FEAT] = r_ref[s]
        early_ref[:, WIDTH + NY * FEAT:EARLY] = jnp.zeros((PY, EARLY - WIDTH - NY * FEAT), BF)
        acc_ref[...] = jnp.zeros_like(acc_ref)

    preact = mm(early_ref[:, 0:WIDTH], win_ref[0])
    hidden = (preact * jax.nn.sigmoid(preact)).astype(BF)
    preact_ref[...] = preact
    early_ref[:, pl.ds(pl.multiple_of(WIDTH + y * FEAT, FEAT), FEAT)] = hidden
    acc_ref[...] += mm(hidden, wout_ref[0])

    @pl.when(y == NY - 1)
    def _():
        send_ref[...] = acc_ref[...].astype(BF)


def proj2_kernel(
    r_ref, target_ref, preact_ref, win_ref, wout_ref, back_ref, late_ref, terms_ref
):
    y = pl.program_id(0)

    @pl.when(y == 0)
    def _():
        proj = r_ref[0].astype(F32)
        for z in range(1, NZ):
            proj = proj + r_ref[z].astype(F32)
        target = target_ref[...]
        scale = 1.0 / TEACH
        cross = jnp.sum(proj * target, axis=1, keepdims=True) * scale
        proj_power = jnp.sum(proj * proj, axis=1, keepdims=True) * scale + EPSILON
        teach_power = jnp.sum(target * target, axis=1, keepdims=True) * scale + EPSILON
        grad = -(target - cross / proj_power * proj) / jnp.sqrt(proj_power * teach_power)
        late_ref[:, 0:TEACH] = grad.astype(BF)
        terms_ref[...] = jnp.zeros_like(terms_ref)

    grad_hidden = mm(late_ref[:, 0:TEACH], wout_ref[0], NT)
    preact = preact_ref[...]
    sigma = jax.nn.sigmoid(preact)
    grad_pre = (grad_hidden * sigma * (1.0 + preact * (1.0 - sigma))).astype(BF)
    terms_ref[...] += mm(grad_pre, win_ref[0], NT)
    late_ref[:, pl.ds(pl.multiple_of(TEACH + y * FEAT, FEAT), FEAT)] = grad_pre

    @pl.when(y == NY - 1)
    def _():
        terms = terms_ref[...].astype(BF)
        for d in range(NS):
            back_ref[d] = terms[:, d * FEAT:(d + 1) * FEAT]


def value_grad_kernel(r_ref, pp_ref, g_ref, *out_refs):
    z = lax.axis_index("seq") % NZ
    for y in range(NY):
        summed = r_ref[y * NZ].astype(F32)
        for k in range(1, NZ):
            summed = summed + r_ref[y * NZ + k].astype(F32)
        rounded = summed.astype(BF).astype(F32) * (1.0 / GROUP)
        g_ref[y * PY:(y + 1) * PY, :] = rounded.astype(BF)
    grad = g_ref[...]
    for k in range(NZ):
        for y in range(NY):
            at = pl.multiple_of((y * NZ + (z + k) % NZ) * TOK, TOK)
            parts = [mm(pp_ref[head, :, pl.ds(at, TOK)], grad, TN) for head in range(2)]
            out_refs[k][y] = jnp.where(low_half((TOK, FEAT)), parts[0], parts[1]).astype(BF)


def turn_grad_kernel(a_ref, b_ref, c_ref, d_ref, *out_refs):
    y = lax.axis_index("seq") // NZ
    for j in range(NY):
        for k, ref in enumerate((a_ref, b_ref, c_ref, d_ref)):
            out_refs[j][k] = ref[(y + j) % NY]


def join_grad_kernel(a_ref, b_ref, c_ref, d_ref, out_ref):
    y = lax.axis_index("seq") // NZ
    z = lax.axis_index("seq") % NZ
    for j, ref in enumerate((a_ref, b_ref, c_ref, d_ref)):
        for k in range(NZ):
            source = (y + NY - j) % NY * NZ + (z + NZ - k) % NZ
            out_ref[0, :, pl.ds(pl.multiple_of(source * FEAT, FEAT), FEAT)] = ref[k]


def bwd_kernel(g_ref, x_ref, v_ref, p_ref, out_ref, d0_ref, d1_ref, w0_ref, w1_ref):
    block = pl.program_id(0)
    step = BBLK // TOK
    keys = x_ref[:, TOK:2 * TOK, :].reshape(LEN, FEAT)
    values = v_ref[...].reshape(LEN, FEAT)
    sel = selector(x_ref, block * step, step)
    upstream = (mm(sel, g_ref[...], TN) * 0.125).astype(BF)
    dprob_refs, work_refs = (d0_ref, d1_ref), (w0_ref, w1_ref)
    for head in range(2):
        dprob_refs[head][...] = mm(of_head(upstream, head), values, NT)
    parts = []
    for head in range(2):
        for c in range(0, BBLK, CHUNK):
            probs = p_ref[head, c:c + CHUNK, :].astype(F32)
            dprob = dprob_refs[head][c:c + CHUNK, :]
            delta = jnp.sum(probs * dprob, axis=1, keepdims=True)
            work_refs[head][c:c + CHUNK, :] = (probs * (dprob - delta)).astype(BF)
        parts.append(mm(work_refs[head][...], keys))
    rows = jnp.where(low_half((BBLK, FEAT)), parts[0], parts[1]).astype(BF)
    out_ref[...] = rows.reshape(step, TOK, FEAT)


def weights_kernel(early_ref, late_ref, out_ref):
    y = lax.axis_index("seq") // NZ
    at = pl.multiple_of(WIDTH + y * FEAT, FEAT)
    hidden = early_ref[:, :, pl.ds(at, FEAT)].reshape(PATCHES, FEAT)
    at = pl.multiple_of(TEACH + y * FEAT, FEAT)
    grad_pre = late_ref[:, :, pl.ds(at, FEAT)].reshape(PATCHES, FEAT)
    pooled = early_ref[:, :, 0:WIDTH].reshape(PATCHES, WIDTH)
    grad = late_ref[:, :, 0:TEACH].reshape(PATCHES, TEACH)
    out_ref[0:WIDTH, :] = mm(pooled, grad_pre, TN).astype(BF)
    grad_out = mm(hidden, grad, TN).astype(BF)
    for c in range(TEACH // FEAT):
        out_ref[WIDTH + c * FEAT:WIDTH + (c + 1) * FEAT, :] = grad_out[:, c * FEAT:(c + 1) * FEAT]


def sum_kernel(r_ref, out_ref):
    total = r_ref[0].astype(F32)
    for k in range(1, r_ref.shape[0]):
        total = total + r_ref[k].astype(F32)
    out_ref[...] = total.astype(BF)


def finish_kernel(r_ref, in_ref, out_ref):
    in_ref[...] = r_ref[0:WIDTH, :].astype(F32)
    for c in range(TEACH // FEAT):
        block = r_ref[WIDTH + c * FEAT:WIDTH + (c + 1) * FEAT, :]
        out_ref[:, c * FEAT:(c + 1) * FEAT] = block.astype(F32)


def unpack_kernel(r_ref, dq_ref):
    for i in range(NS // PARTS):
        dq_ref[0, :, i * FEAT:(i + 1) * FEAT] = r_ref[i]


def exchange(array, axis, groups=None):
    return lax.all_to_all(array, axis, 0, 0, axis_index_groups=groups, tiled=True)


def gather(array, axis, groups=None):
    return lax.all_gather(array, axis, axis=0, axis_index_groups=groups, tiled=False)


def fixed(shape):
    return pl.BlockSpec(shape, lambda i: (0,) * len(shape))


def per_device(query, key, value, patch_map, teacher, proj_in, proj_out):
    win = gather(proj_in, "seq", Y_GROUPS)
    wout = gather(proj_out, "seq", Y_GROUPS)
    columns = pl.BlockSpec((1, TOK, WIDTH // PARTS), lambda i: (0, 0, i))
    chunk = lambda rows: pl.BlockSpec((NS // PARTS, rows, FEAT), lambda i: (i, 0, 0))

    packed = pl.pallas_call(
        pack_kernel,
        grid=(PARTS,),
        out_shape=sds((NS, ROWS, FEAT), BF),
        in_specs=[columns, columns, fixed((1, TOK))],
        out_specs=chunk(ROWS),
        compiler_params=params(59),
    )(query, key, patch_map)
    packed, value, teacher = lax.optimization_barrier((packed, value, teacher))
    x = exchange(packed, "seq")
    pieces = pl.pallas_call(
        split_value_kernel,
        out_shape=(sds((NZ, TOK, FEAT), BF),) * NY,
        in_specs=whole(1),
        out_specs=tuple(whole(NY)),
        compiler_params=params(),
    )(value)
    pieces = [pieces[0]] + [lax.ppermute(pieces[k], "seq", Y_SHIFT[k]) for k in range(1, NY)]
    turned = pl.pallas_call(
        turn_value_kernel,
        out_shape=(sds((TROWS + NY * TOK, FEAT), BF),) * NZ,
        in_specs=whole(5),
        out_specs=tuple(whole(NZ)),
        compiler_params=params(),
    )(*pieces, teacher)
    turned = [turned[0]] + [lax.ppermute(turned[k], "seq", Z_SHIFT[k]) for k in range(1, NZ)]

    probs, pooled_probs = pl.pallas_call(
        fwd_kernel,
        grid=(LEN // FBLK,),
        out_shape=(sds((2, LEN, LEN), BF), sds((2, PATCHES, LEN), BF)),
        in_specs=[fixed((NS, ROWS, FEAT))],
        out_specs=(
            pl.BlockSpec((2, FBLK, LEN), lambda i: (0, i, 0)),
            fixed((2, PATCHES, LEN)),
        ),
        scratch_shapes=[
            pltpu.VMEM((2, PATCHES, LEN), F32),
            pltpu.VMEM((FBLK, LEN), F32),
            pltpu.VMEM((FBLK, LEN), F32),
        ],
        compiler_params=params(40),
        cost_estimate=pl.CostEstimate(flops=10 ** 6, bytes_accessed=10 ** 6, transcendentals=0),
    )(x)
    pooled_out, values, targets = pl.pallas_call(
        pool_kernel,
        out_shape=(sds((NS, PY, FEAT), BF), sds((NS, TOK, FEAT), BF), sds((PY, TEACH), F32)),
        in_specs=whole(5),
        out_specs=tuple(whole(3)),
        compiler_params=params(),
    )(pooled_probs, *turned)
    pooled_in = exchange(pooled_out, "seq")

    win_spec = pl.BlockSpec((1, WIDTH, FEAT), lambda i: (i, 0, 0))
    wout_spec = pl.BlockSpec((1, FEAT, TEACH), lambda i: (i, 0, 0))
    slab = pl.BlockSpec((PY, FEAT), lambda i: (0, i))
    early, preact, partial = pl.pallas_call(
        proj1_kernel,
        grid=(NY,),
        out_shape=(sds((PY, EARLY), BF), sds((PY, NY * FEAT), F32), sds((PY, TEACH), BF)),
        in_specs=[fixed((NS, PY, FEAT)), win_spec, wout_spec],
        out_specs=(fixed((PY, EARLY)), slab, fixed((PY, TEACH))),
        scratch_shapes=[pltpu.VMEM((PY, TEACH), F32)],
        compiler_params=params(59),
    )(pooled_in, win, wout)
    early_in = gather(early, "seq", Y_GROUPS)
    partials = gather(partial, "seq", Z_GROUPS)

    back, late = pl.pallas_call(
        proj2_kernel,
        grid=(NY,),
        out_shape=(sds((NS, PY, FEAT), BF), sds((PY, LATE), BF)),
        in_specs=[fixed((NZ, PY, TEACH)), fixed((PY, TEACH)), slab, win_spec, wout_spec],
        out_specs=(fixed((NS, PY, FEAT)), fixed((PY, LATE))),
        scratch_shapes=[pltpu.VMEM((PY, WIDTH), F32)],
        compiler_params=params(),
    )(partials, targets, preact, win, wout)
    back_in = exchange(back, "seq")
    late_in = gather(late, "seq", Y_GROUPS)

    terms = pl.pallas_call(
        weights_kernel,
        out_shape=sds((WIDTH + TEACH, FEAT), BF),
        in_specs=whole(2),
        out_specs=whole(1)[0],
        compiler_params=params(),
    )(early_in, late_in)
    terms, back_in = lax.optimization_barrier((terms, back_in))
    part = exchange(terms.reshape(8, ROWS_DP, FEAT), "dp", XC_GROUPS)

    grad_rows, *moved = pl.pallas_call(
        value_grad_kernel,
        out_shape=(sds((PATCHES, FEAT), BF),) + (sds((NY, TOK, FEAT), BF),) * NZ,
        in_specs=whole(2),
        out_specs=tuple(whole(1 + NZ)),
        compiler_params=params(),
    )(back_in, pooled_probs)
    moved = [moved[0]] + [lax.ppermute(moved[k], "seq", Z_SHIFT[k]) for k in range(1, NZ)]
    grads = pl.pallas_call(
        bwd_kernel,
        grid=(LEN // BBLK,),
        out_shape=sds((NS, TOK, FEAT), BF),
        in_specs=[
            fixed((PATCHES, FEAT)),
            fixed((NS, ROWS, FEAT)),
            fixed((NS, TOK, FEAT)),
            pl.BlockSpec((2, BBLK, LEN), lambda i: (0, i, 0)),
        ],
        out_specs=pl.BlockSpec((BBLK // TOK, TOK, FEAT), lambda i: (i, 0, 0)),
        scratch_shapes=[
            pltpu.VMEM((BBLK, LEN), F32),
            pltpu.VMEM((BBLK, LEN), F32),
            pltpu.VMEM((BBLK, LEN), BF),
            pltpu.VMEM((BBLK, LEN), BF),
        ],
        compiler_params=params(50),
        cost_estimate=pl.CostEstimate(flops=10 ** 10, bytes_accessed=2 * 10 ** 7, transcendentals=0),
    )(grad_rows, x, values, probs)
    turned = pl.pallas_call(
        turn_grad_kernel,
        out_shape=(sds((NZ, TOK, FEAT), BF),) * NY,
        in_specs=whole(NZ),
        out_specs=tuple(whole(NY)),
        compiler_params=params(),
    )(*moved)
    turned, grads = lax.optimization_barrier((turned, grads))
    turned = [turned[0]] + [lax.ppermute(turned[k], "seq", Y_SHIFT[k]) for k in range(1, NY)]
    grad_value = pl.pallas_call(
        join_grad_kernel,
        out_shape=sds((1, TOK, WIDTH), BF),
        in_specs=whole(NY),
        out_specs=whole(1)[0],
        compiler_params=params(),
    )(*turned)
    part, grads = lax.optimization_barrier((part, grads))
    part = pl.pallas_call(
        sum_kernel,
        out_shape=sds((ROWS_DP, FEAT), BF),
        in_specs=whole(1),
        out_specs=whole(1)[0],
        compiler_params=params(),
    )(part)
    part = gather(part, "dp", ZL_GROUPS)
    part, grads = lax.optimization_barrier((part, grads))
    grads_in = exchange(grads, "seq")
    part = pl.pallas_call(
        sum_kernel,
        out_shape=sds((ROWS_DP, FEAT), BF),
        in_specs=whole(1),
        out_specs=whole(1)[0],
        compiler_params=params(),
    )(part)
    total = gather(part, "dp", XC_GROUPS).reshape(WIDTH + TEACH, FEAT)
    grad_in, grad_out = pl.pallas_call(
        finish_kernel,
        out_shape=(sds((WIDTH, FEAT), F32), sds((FEAT, TEACH), F32)),
        in_specs=whole(1),
        out_specs=tuple(whole(2)),
        compiler_params=params(),
    )(total)

    grad_query = pl.pallas_call(
        unpack_kernel,
        grid=(PARTS,),
        out_shape=sds((1, TOK, WIDTH), BF),
        in_specs=[chunk(TOK)],
        out_specs=columns,
        compiler_params=params(),
    )(grads_in)
    return (grad_query, grad_value, grad_in, grad_out)


def solution(mesh):
    placed = (
        P("dp", "seq", None),
        P("dp", "seq", None),
        P("dp", "seq", None),
        P("dp", "seq"),
        P("dp", "seq", None),
        P(None, "seq"),
        P("seq", None),
    )
    return jax.shard_map(
        per_device,
        mesh=mesh,
        in_specs=placed,
        out_specs=(P("dp", "seq", None), P("dp", "seq", None), P(None, "seq"), P("seq", None)),
        check_vma=False,
    )
```

time: 348 us -> 305 us (0.88)
  starting transfers between devices: 42.9 us -> 115 us
  blocking collectives: 127 us -> 63.6 us
  waiting for transfers between devices: 106 us -> 56.1 us
    all_to_all x5, waiting for transfers between devices: 105 us -> 29.6 us  [exchange(): lax.all_to_all(array, axis, 0, 0, axis_index_groups=groups, tiled=True)]
    ppermute x0 -> x12, starting transfers between devices: none -> 67 us  [the longest x3 25.2 us: per_device(): lax.ppermute(turned[k], 'seq', Z_SHIFT[k])]
    all_to_all x2 -> x0, blocking collectives: 37.7 us -> none  [exchange(): lax.all_to_all(array, axis, 0, 0, axis_index_groups=groups, tiled=True)]
    all_gather x3 -> x4, blocking collectives: 89.3 us -> 63.6 us  [gather(): lax.all_gather(array, axis, axis=0, axis_index_groups=groups, tiled=False)]
    ppermute x0 -> x12, waiting for transfers between devices: none -> 25 us  [the longest x3 13.1 us: per_device(): lax.ppermute(pieces[k], 'seq', Y_SHIFT[k])]
    all_to_all x5, starting transfers between devices: 42.9 us -> 48 us  [exchange(): lax.all_to_all(array, axis, 0, 0, axis_index_groups=groups, tiled=True)]
    pallas_call x6 -> x15, Pallas kernels: 45.7 us -> 46.6 us  [the longest x1 15.5 us: per_device(): pl.pallas_call(bwd_kernel, grid=(LEN // BBLK,), out_shape=sds((NS, TOK, F...]
    unnamed x18 -> x34, local copies, waits for them, and re-layouts: 7.89 us -> 7.43 us
  transfers between devices with their start and end apart: 7 -> 20, of which waited for: 3 -> 9; matrix products, arithmetic and copies ran while one was open for 1% -> 0% of each run, Pallas kernels for 11% -> 14%
where the time goes in v2:
time: 305 us; the launch traced here: 304 us
  starting transfers between devices  115 us (38%)
  blocking collectives  63.6 us (21%)
  waiting for transfers between devices  56.1 us (18%)
  Pallas kernels  48 us (16%)
  between operations  14 us (5%)
  local copies, waits for them, and re-layouts  7.43 us (2%)
    all_gather x4, blocking collectives, gather(): lax.all_gather(array, axis, axis=0, axis_index_groups=groups, tiled=False)  63.6 us
    all_to_all x5, starting transfers between devices, exchange(): lax.all_to_all(array, axis, 0, 0, axis_index_groups=groups, tiled=True)  48 us
    all_to_all x5, waiting for transfers between devices, exchange(): lax.all_to_all(array, axis, 0, 0, axis_index_groups=groups, tiled=True)  29.6 us
    ppermute x3, starting transfers between devices, per_device(): lax.ppermute(turned[k], 'seq', Z_SHIFT[k])  25.2 us
    ppermute x3, starting transfers between devices, per_device(): lax.ppermute(moved[k], 'seq', Z_SHIFT[k])  21.1 us
    pallas_call x1, Pallas kernels, per_device(): pl.pallas_call(bwd_kernel, grid=(LEN // BBLK,), out_shape=sds((NS, TOK, F...  15.5 us
    pallas_call x1, Pallas kernels, per_device(): pl.pallas_call(fwd_kernel, grid=(LEN // FBLK,), out_shape=(sds((2, LEN, L...  14.5 us
    ppermute x3, waiting for transfers between devices, per_device(): lax.ppermute(pieces[k], 'seq', Y_SHIFT[k])  13.1 us
  transfers between devices with their start and end apart: 20, of which 9 were waited for; matrix products, arithmetic and copies ran while one was open for 0% of the time, Pallas kernels for 14%

profile of v2, /device:TPU:1, one launch (start us, length us, event | category | flops | bytes accessed | tf_op | source)
XLA Modules:
  0.0 304.3 jit_solution(17556483503256495211)
XLA Ops:
  7.2 0.7 all-gather.13.cloned.1.call-update
  7.9 3.5 %shard_map.102 = bf16[16,272,128]{2,1,0:T(8,128)(2,1)} custom-call(bf16[1,128,2048]{2,1,0:T(8,128)(2,1)} %q_ref.1, bf16[1,128,2048]{2,1,0:T(8,128)(2,1)} %k_ref.1, s32[1,128]{1,0:T(1,128)} %ids_ref.1), custom_call_target="tpu_custom_call" | custom-call | tf_op jit(solution)/shard_map/pallas_call | solution.py:321
  11.4 18.5 %all-to-all-start = ((bf16[16,272,128]{2,1,0:T(8,128)(2,1)}), bf16[16,272,128]{2,1,0:T(8,128)(2,1)S(1)}, u32[]{:S(2)}, u32[]{:S(2)}) async-start(bf16[16,272,128]{2,1,0:T(8,128)(2,1)} %shard_map.102), calls=%async_computation | async-start | bytes 2228224 | tf_op jit(solution)/shard_map/all_to_all | solution.py:304
  30.0 0.7 all-gather.11.cloned.1.call-update
  30.8 3.3 %collective-permute-start = (bf16[4,128,128]{2,1,0:T(8,128)(2,1)S(1)}, bf16[4,128,128]{2,1,0:T(8,128)(2,1)S(1)}, u32[]{:S(2)}, u32[]{:S(2)}) collective-permute-start(bf16[4,128,128]{2,1,0:T(8,128)(2,1)S(1)} %get-tuple-element.51), channel_id=1, source_target_pairs={{0,4},{1,5},{2,6},{3,7},{4,8},{5,9},{6,10},{7,11},{8,12},{9,13},{1... | collective-permute-start | bytes 393224 | tf_op jit(solution)/shard_map/ppermute | solution.py:338
  34.1 4.3 %collective-permute-start.1 = (bf16[4,128,128]{2,1,0:T(8,128)(2,1)S(1)}, bf16[4,128,128]{2,1,0:T(8,128)(2,1)S(1)}, u32[]{:S(2)}, u32[]{:S(2)}) collective-permute-start(bf16[4,128,128]{2,1,0:T(8,128)(2,1)S(1)} %get-tuple-element.52), channel_id=1, source_target_pairs={{0,8},{1,9},{2,10},{3,11},{4,12},{5,13},{6,14},{7,15},{8,0},{9,1},... | collective-permute-start | bytes 393224 | tf_op jit(solution)/shard_map/ppermute | solution.py:338
  38.4 3.1 %collective-permute-start.2 = (bf16[4,128,128]{2,1,0:T(8,128)(2,1)S(1)}, bf16[4,128,128]{2,1,0:T(8,128)(2,1)S(1)}, u32[]{:S(2)}, u32[]{:S(2)}) collective-permute-start(bf16[4,128,128]{2,1,0:T(8,128)(2,1)S(1)} %get-tuple-element.53), channel_id=1, source_target_pairs={{0,12},{1,13},{2,14},{3,15},{4,0},{5,1},{6,2},{7,3},{8,4},{9,5},{1... | collective-permute-start | bytes 393224 | tf_op jit(solution)/shard_map/ppermute | solution.py:338
  41.5 2.0 collective-permute-done.b_ref
  43.5 9.5 %collective-permute-done.1.c_ref = bf16[4,128,128]{2,1,0:T(8,128)(2,1)S(1)} collective-permute-done((bf16[4,128,128]{2,1,0:T(8,128)(2,1)S(1)}, bf16[4,128,128]{2,1,0:T(8,128)(2,1)S(1)}, u32[]{:S(2)}, u32[]{:S(2)}) %collective-permute-start.1) | collective-permute-done | bytes 131104 | tf_op jit(solution)/shard_map/ppermute | solution.py:338
  53.1 1.6 collective-permute-done.2.d_ref
  54.7 7.9 %collective-permute-start.3 = (bf16[608,128]{1,0:T(8,128)(2,1)S(1)}, bf16[608,128]{1,0:T(8,128)(2,1)S(1)}, u32[]{:S(2)}, u32[]{:S(2)}) collective-permute-start(bf16[608,128]{1,0:T(8,128)(2,1)S(1)} %get-tuple-element.56), channel_id=1, source_target_pairs={{0,1},{1,2},{2,3},{3,0},{4,5},{5,6},{6,7},{7,4},{8,9},{9,10},{10,1... | collective-permute-start | bytes 466952 | tf_op jit(solution)/shard_map/ppermute | solution.py:346
  62.7 10.0 %collective-permute-start.4 = (bf16[608,128]{1,0:T(8,128)(2,1)S(1)}, bf16[608,128]{1,0:T(8,128)(2,1)S(1)}, u32[]{:S(2)}, u32[]{:S(2)}) collective-permute-start(bf16[608,128]{1,0:T(8,128)(2,1)S(1)} %get-tuple-element.57), channel_id=1, source_target_pairs={{0,2},{1,3},{2,0},{3,1},{4,6},{5,7},{6,4},{7,5},{8,10},{9,11},{10,... | collective-permute-start | bytes 466952 | tf_op jit(solution)/shard_map/ppermute | solution.py:346
  72.7 7.3 %collective-permute-start.5 = (bf16[608,128]{1,0:T(8,128)(2,1)S(1)}, bf16[608,128]{1,0:T(8,128)(2,1)S(1)}, u32[]{:S(2)}, u32[]{:S(2)}) collective-permute-start(bf16[608,128]{1,0:T(8,128)(2,1)S(1)} %get-tuple-element.58), channel_id=1, source_target_pairs={{0,3},{1,0},{2,1},{3,2},{4,7},{5,4},{6,5},{7,6},{8,11},{9,8},{10,9... | collective-permute-start | bytes 466952 | tf_op jit(solution)/shard_map/ppermute | solution.py:346
  79.9 13.6 %all-to-all-done.x_ref = bf16[16,272,128]{2,1,0:T(8,128)(2,1)S(1)} async-done(((bf16[16,272,128]{2,1,0:T(8,128)(2,1)}), bf16[16,272,128]{2,1,0:T(8,128)(2,1)S(1)}, u32[]{:S(2)}, u32[]{:S(2)}) %all-to-all-start) | async-done | bytes 1114144 | tf_op jit(solution)/shard_map/all_to_all | solution.py:304
  93.6 14.5 %shard_map.103 = (bf16[2,2048,2048]{2,1,0:T(8,128)(2,1)}, bf16[2,128,2048]{2,1,0:T(8,128)(2,1)S(1)}) custom-call(bf16[16,272,128]{2,1,0:T(8,128)(2,1)S(1)} %all-to-all-done.x_ref), custom_call_target="tpu_custom_call" | custom-call | flops 1000000 | bytes 1000000 | tf_op jit(solution)/shard_map/pallas_call | solution.py:348
  108.1 6.6 %collective-permute-done.4.c_ref = bf16[608,128]{1,0:T(8,128)(2,1)S(1)} collective-permute-done((bf16[608,128]{1,0:T(8,128)(2,1)S(1)}, bf16[608,128]{1,0:T(8,128)(2,1)S(1)}, u32[]{:S(2)}, u32[]{:S(2)}) %collective-permute-start.4) | collective-permute-done | bytes 155680 | tf_op jit(solution)/shard_map/ppermute | solution.py:346
  114.7 1.2 shard_map.106
  115.8 1.0 copy-done.4
  116.8 0.7 copy-done.8
  117.4 0.8 copy-done.14
  118.2 5.9 %all-to-all-start.1 = ((bf16[16,32,128]{2,1,0:T(8,128)(2,1)}), bf16[16,32,128]{2,1,0:T(8,128)(2,1)S(1)}, u32[]{:S(2)}, u32[]{:S(2)}) async-start(bf16[16,32,128]{2,1,0:T(8,128)(2,1)} %get-tuple-element.59), calls=%async_computation.1 | async-start | bytes 262144 | tf_op jit(solution)/shard_map/all_to_all | solution.py:304
  124.2 15.5 %all-to-all-done.1.r_ref = bf16[16,32,128]{2,1,0:T(8,128)(2,1)S(1)} async-done(((bf16[16,32,128]{2,1,0:T(8,128)(2,1)}), bf16[16,32,128]{2,1,0:T(8,128)(2,1)S(1)}, u32[]{:S(2)}, u32[]{:S(2)}) %all-to-all-start.1) | async-done | bytes 131104 | tf_op jit(solution)/shard_map/all_to_all | solution.py:304
  139.7 0.7 copy-done.16
  140.3 4.8 %shard_map.107 = (bf16[32,4224]{1,0:T(8,128)(2,1)}, f32[32,512]{1,0:T(8,128)}, bf16[32,1408]{1,0:T(8,128)(2,1)}) custom-call(bf16[16,32,128]{2,1,0:T(8,128)(2,1)} %copy-done.16, bf16[4,2048,128]{2,1,0:T(8,128)(2,1)} %bitcast.7, bf16[4,128,1408]{2,1,0:T(8,128)(2,1)} %bitcast.9), custom_call_target="tpu_custom_call" | custom-call | tf_op jit(solution)/shard_map/pallas_call | solution.py:377
  145.2 15.7 %all-gather.3 = bf16[128,1408]{1,0:T(8,128)(2,1)S(1)} all-gather(bf16[32,1408]{1,0:T(8,128)(2,1)} %get-tuple-element.61), channel_id=5, replica_groups={{0,1,2,3},{4,5,6,7},{8,9,10,11},{12,13,14,15},{16,17,18,19},{20,21,22,2..., dimensions={0}, use_global_device_ids=true | all-gather | bytes 450560 | tf_op jit(solution)/shard_map/all_gather | solution.py:308
  160.9 0.9 copy-done.9
  161.8 0.8 copy-done.12
  162.6 2.6 shard_map.108
  166.5 7.2 %all-to-all-start.2 = ((bf16[16,32,128]{2,1,0:T(8,128)(2,1)}), bf16[16,32,128]{2,1,0:T(8,128)(2,1)S(1)}, u32[]{:S(2)}, u32[]{:S(2)}) async-start(bf16[16,32,128]{2,1,0:T(8,128)(2,1)} %copy-done.10), calls=%async_computation.2 | async-start | bytes 262144 | tf_op jit(solution)/shard_map/all_to_all | solution.py:304
  173.7 11.2 %all-gather.4 = bf16[128,1920]{1,0:T(8,128)(2,1)S(1)} all-gather(bf16[32,1920]{1,0:T(8,128)(2,1)} %copy-done.11), channel_id=6, replica_groups={{0,4,8,12},{1,5,9,13},{2,6,10,14},{3,7,11,15},{16,20,24,28},{17,21,25,2..., dimensions={0}, use_global_device_ids=true | all-gather | bytes 614400 | tf_op jit(solution)/shard_map/all_gather | solution.py:308
  185.0 1.2 copy-done.6
  186.2 1.4 shard_map.109
  188.6 6.9 %collective-permute-start.6 = (bf16[4,128,128]{2,1,0:T(8,128)(2,1)S(1)}, bf16[4,128,128]{2,1,0:T(8,128)(2,1)S(1)}, u32[]{:S(2)}, u32[]{:S(2)}) collective-permute-start(bf16[4,128,128]{2,1,0:T(8,128)(2,1)S(1)} %get-tuple-element.69), channel_id=1, source_target_pairs={{0,1},{1,2},{2,3},{3,0},{4,5},{5,6},{6,7},{7,4},{8,9},{9,10},{10,1... | collective-permute-start | bytes 393224 | tf_op jit(solution)/shard_map/ppermute | solution.py:418
  195.6 6.9 %collective-permute-start.7 = (bf16[4,128,128]{2,1,0:T(8,128)(2,1)S(1)}, bf16[4,128,128]{2,1,0:T(8,128)(2,1)S(1)}, u32[]{:S(2)}, u32[]{:S(2)}) collective-permute-start(bf16[4,128,128]{2,1,0:T(8,128)(2,1)S(1)} %get-tuple-element.70), channel_id=1, source_target_pairs={{0,2},{1,3},{2,0},{3,1},{4,6},{5,7},{6,4},{7,5},{8,10},{9,11},{10,... | collective-permute-start | bytes 393224 | tf_op jit(solution)/shard_map/ppermute | solution.py:418
  202.5 7.3 %collective-permute-start.8 = (bf16[4,128,128]{2,1,0:T(8,128)(2,1)S(1)}, bf16[4,128,128]{2,1,0:T(8,128)(2,1)S(1)}, u32[]{:S(2)}, u32[]{:S(2)}) collective-permute-start(bf16[4,128,128]{2,1,0:T(8,128)(2,1)S(1)} %get-tuple-element.71), channel_id=1, source_target_pairs={{0,3},{1,0},{2,1},{3,2},{4,7},{5,4},{6,5},{7,6},{8,11},{9,8},{10,9... | collective-permute-start | bytes 393224 | tf_op jit(solution)/shard_map/ppermute | solution.py:418
  209.7 12.8 %all-to-all-start.3 = ((bf16[8,432,128]{2,1,0:T(8,128)(2,1)}), bf16[8,432,128]{2,1,0:T(8,128)(2,1)S(1)}, u32[]{:S(2)}, u32[]{:S(2)}) async-start(bf16[8,432,128]{2,1,0:T(8,128)(2,1)} %bitcast.5), calls=%async_computation.3 | async-start | bytes 1769472 | tf_op jit(solution)/shard_map/all_to_all | solution.py:304
  222.6 15.5 %shard_map.112 = bf16[16,128,128]{2,1,0:T(8,128)(2,1)} custom-call(bf16[128,128]{1,0:T(8,128)(2,1)S(1)} %get-tuple-element.76.g_ref, bf16[16,272,128]{2,1,0:T(8,128)(2,1)S(1)} %copy-done.3, bf16[16,128,128]{2,1,0:T(8,128)(2,1)S(1)} %copy-done.15, bf16[2,2048,2048]{2,1,0:T(8,128)(2,1)} %get-tuple-element.78.p_ref), custom_call_target="tpu_custom_call" | custom-call | flops 10000000000 | bytes 20000000 | tf_op jit(solution)/shard_map/pallas_call | solution.py:419
  238.3 19.4 %all-gather.5 = bf16[1728,128]{1,0:T(8,128)(2,1)S(1)} all-gather(bf16[432,128]{1,0:T(8,128)(2,1)S(1)} %shard_map.113), channel_id=7, replica_groups={{0,32,64,96},{16,48,80,112},{128,160,192,224},{144,176,208,240},{256,28..., dimensions={0}, use_global_device_ids=true | all-gather | bytes 552960 | tf_op jit(solution)/shard_map/all_gather | solution.py:308
  257.7 3.7 %all-to-all-start.4 = ((bf16[16,128,128]{2,1,0:T(8,128)(2,1)}), bf16[16,128,128]{2,1,0:T(8,128)(2,1)S(1)}, u32[]{:S(2)}, u32[]{:S(2)}) async-start(bf16[16,128,128]{2,1,0:T(8,128)(2,1)} %shard_map.112), calls=%async_computation.4 | async-start | bytes 1048576 | tf_op jit(solution)/shard_map/all_to_all | solution.py:304
  261.4 4.8 %collective-permute-start.10 = (bf16[4,128,128]{2,1,0:T(8,128)(2,1)S(1)}, bf16[4,128,128]{2,1,0:T(8,128)(2,1)S(1)}, u32[]{:S(2)}, u32[]{:S(2)}) collective-permute-start(bf16[4,128,128]{2,1,0:T(8,128)(2,1)S(1)} %get-tuple-element.85), channel_id=1, source_target_pairs={{0,8},{1,9},{2,10},{3,11},{4,12},{5,13},{6,14},{7,15},{8,0},{9,1},... | collective-permute-start | bytes 393224 | tf_op jit(solution)/shard_map/ppermute | solution.py:447
  266.1 2.8 collective-permute-start.11
  268.9 2.5 collective-permute-start.9
  271.4 2.5 collective-permute-done.11.d_ref
  273.9 2.8 collective-permute-done.9.b_ref
  276.8 0.9 shard_map.115
  277.8 17.3 %all-gather.6.r_ref = bf16[3456,128]{1,0:T(8,128)(2,1)S(1)} all-gather(bf16[432,128]{1,0:T(8,128)(2,1)S(1)} %shard_map.116), channel_id=8, replica_groups={{0,16,128,144,256,272,384,400},{32,48,160,176,288,304,416,432},{64,80,1..., dimensions={0}, use_global_device_ids=true | all-gather | bytes 995328 | tf_op jit(solution)/shard_map/all_gather | solution.py:308
  295.1 1.3 shard_map.117
  296.3 1.4 shard_map.114
  (49 shorter events, 3.0 us)
Async XLA Ops:
  7.2 117.0 %all-gather.13.cloned.1.call-start = ((), (), s32[]{:S(2)}) async-start(), calls=%async_computation.6 | async-start | bytes 1802240 | tf_op jit(solution)/shard_map/all_gather | solution.py:308
  11.4 19.3 %copy-start.7 = (bf16[1,128,2048]{2,1,0:T(8,128)(2,1)S(1)}, bf16[1,128,2048]{2,1,0:T(8,128)(2,1)}, u32[]{:S(2)}) copy-start(bf16[1,128,2048]{2,1,0:T(8,128)(2,1)} %v_ref) | copy-start | bytes 1572868
  11.4 43.3 %copy-start.13 = (bf16[1,8,1408]{2,1,0:T(8,128)(2,1)S(1)}, bf16[1,8,1408]{2,1,0:T(8,128)(2,1)}, u32[]{:S(2)}) copy-start(bf16[1,8,1408]{2,1,0:T(8,128)(2,1)} %teacher_ref) | copy-start | bytes 67588
  11.4 82.2 %all-to-all-start = ((bf16[16,272,128]{2,1,0:T(8,128)(2,1)}), bf16[16,272,128]{2,1,0:T(8,128)(2,1)S(1)}, u32[]{:S(2)}, u32[]{:S(2)}) async-start(bf16[16,272,128]{2,1,0:T(8,128)(2,1)} %shard_map.102), calls=%async_computation | async-start | bytes 2228224 | tf_op jit(solution)/shard_map/all_to_all | solution.py:304
  29.9 94.3 %all-gather.11.cloned.1.call-start = ((), (), s32[]{:S(2)}) async-start(), calls=%async_computation.5 | async-start | bytes 2621440 | tf_op jit(solution)/shard_map/all_gather | solution.py:308
  30.8 12.7 %collective-permute-start = (bf16[4,128,128]{2,1,0:T(8,128)(2,1)S(1)}, bf16[4,128,128]{2,1,0:T(8,128)(2,1)S(1)}, u32[]{:S(2)}, u32[]{:S(2)}) collective-permute-start(bf16[4,128,128]{2,1,0:T(8,128)(2,1)S(1)} %get-tuple-element.51), channel_id=1, source_target_pairs={{0,4},{1,5},{2,6},{3,7},{4,8},{5,9},{6,10},{7,11},{8,12},{9,13},{1... | collective-permute-start | bytes 393224 | tf_op jit(solution)/shard_map/ppermute | solution.py:338
  34.1 19.0 %collective-permute-start.1 = (bf16[4,128,128]{2,1,0:T(8,128)(2,1)S(1)}, bf16[4,128,128]{2,1,0:T(8,128)(2,1)S(1)}, u32[]{:S(2)}, u32[]{:S(2)}) collective-permute-start(bf16[4,128,128]{2,1,0:T(8,128)(2,1)S(1)} %get-tuple-element.52), channel_id=1, source_target_pairs={{0,8},{1,9},{2,10},{3,11},{4,12},{5,13},{6,14},{7,15},{8,0},{9,1},... | collective-permute-start | bytes 393224 | tf_op jit(solution)/shard_map/ppermute | solution.py:338
  38.4 16.2 %collective-permute-start.2 = (bf16[4,128,128]{2,1,0:T(8,128)(2,1)S(1)}, bf16[4,128,128]{2,1,0:T(8,128)(2,1)S(1)}, u32[]{:S(2)}, u32[]{:S(2)}) collective-permute-start(bf16[4,128,128]{2,1,0:T(8,128)(2,1)S(1)} %get-tuple-element.53), channel_id=1, source_target_pairs={{0,12},{1,13},{2,14},{3,15},{4,0},{5,1},{6,2},{7,3},{8,4},{9,5},{1... | collective-permute-start | bytes 393224 | tf_op jit(solution)/shard_map/ppermute | solution.py:338
  54.7 53.4 %collective-permute-start.3 = (bf16[608,128]{1,0:T(8,128)(2,1)S(1)}, bf16[608,128]{1,0:T(8,128)(2,1)S(1)}, u32[]{:S(2)}, u32[]{:S(2)}) collective-permute-start(bf16[608,128]{1,0:T(8,128)(2,1)S(1)} %get-tuple-element.56), channel_id=1, source_target_pairs={{0,1},{1,2},{2,3},{3,0},{4,5},{5,6},{6,7},{7,4},{8,9},{9,10},{10,1... | collective-permute-start | bytes 466952 | tf_op jit(solution)/shard_map/ppermute | solution.py:346
  62.7 52.0 %collective-permute-start.4 = (bf16[608,128]{1,0:T(8,128)(2,1)S(1)}, bf16[608,128]{1,0:T(8,128)(2,1)S(1)}, u32[]{:S(2)}, u32[]{:S(2)}) collective-permute-start(bf16[608,128]{1,0:T(8,128)(2,1)S(1)} %get-tuple-element.57), channel_id=1, source_target_pairs={{0,2},{1,3},{2,0},{3,1},{4,6},{5,7},{6,4},{7,5},{8,10},{9,11},{10,... | collective-permute-start | bytes 466952 | tf_op jit(solution)/shard_map/ppermute | solution.py:346
  72.7 42.0 %collective-permute-start.5 = (bf16[608,128]{1,0:T(8,128)(2,1)S(1)}, bf16[608,128]{1,0:T(8,128)(2,1)S(1)}, u32[]{:S(2)}, u32[]{:S(2)}) collective-permute-start(bf16[608,128]{1,0:T(8,128)(2,1)S(1)} %get-tuple-element.58), channel_id=1, source_target_pairs={{0,3},{1,0},{2,1},{3,2},{4,7},{5,4},{6,5},{7,6},{8,11},{9,8},{10,9... | collective-permute-start | bytes 466952 | tf_op jit(solution)/shard_map/ppermute | solution.py:346
  93.6 24.7 %copy-start.2 = (bf16[16,272,128]{2,1,0:T(8,128)(2,1)}, bf16[16,272,128]{2,1,0:T(8,128)(2,1)S(1)}, u32[]{:S(2)}) copy-start(bf16[16,272,128]{2,1,0:T(8,128)(2,1)S(1)} %all-to-all-done.x_ref) | copy-start | bytes 3342340
  115.8 1.0 copy-start.4
  116.8 0.7 copy-start.8
  117.4 0.8 copy-start.14
  118.2 21.4 %all-to-all-start.1 = ((bf16[16,32,128]{2,1,0:T(8,128)(2,1)}), bf16[16,32,128]{2,1,0:T(8,128)(2,1)S(1)}, u32[]{:S(2)}, u32[]{:S(2)}) async-start(bf16[16,32,128]{2,1,0:T(8,128)(2,1)} %get-tuple-element.59), calls=%async_computation.1 | async-start | bytes 262144 | tf_op jit(solution)/shard_map/all_to_all | solution.py:304
  124.1 60.9 %all-gather.15.cloned.1.call-start = ((), (), s32[]{:S(2)}) async-start(), calls=%async_computation.7 | async-start | bytes 1351680 | tf_op jit(solution)/shard_map/all_gather | solution.py:308
  139.7 0.7 copy-start.16
  140.3 20.5 %copy-start = (bf16[8192,128]{1,0:T(8,128)(2,1)S(1)}, bf16[8192,128]{1,0:T(8,128)(2,1)}, u32[]{:S(2)}) copy-start(bf16[8192,128]{1,0:T(8,128)(2,1)} %all-gather.11.cloned.1.call-done) | copy-start | bytes 6291460
  140.3 20.5 %copy-start.1 = (bf16[512,1408]{1,0:T(8,128)(2,1)S(1)}, bf16[512,1408]{1,0:T(8,128)(2,1)}, u32[]{:S(2)}) copy-start(bf16[512,1408]{1,0:T(8,128)(2,1)} %all-gather.13.cloned.1.call-done) | copy-start | bytes 4325380
  160.9 0.9 copy-start.9
  161.8 0.8 copy-start.12
  165.2 0.7 copy-start.10
  165.9 0.6 copy-start.11
  166.5 21.6 %all-to-all-start.2 = ((bf16[16,32,128]{2,1,0:T(8,128)(2,1)}), bf16[16,32,128]{2,1,0:T(8,128)(2,1)S(1)}, u32[]{:S(2)}, u32[]{:S(2)}) async-start(bf16[16,32,128]{2,1,0:T(8,128)(2,1)} %copy-done.10), calls=%async_computation.2 | async-start | bytes 262144 | tf_op jit(solution)/shard_map/all_to_all | solution.py:304
  173.7 14.4 %copy-start.5 = (bf16[2,128,2048]{2,1,0:T(8,128)(2,1)S(1)}, bf16[2,128,2048]{2,1,0:T(8,128)(2,1)}, u32[]{:S(2)}) copy-start(bf16[2,128,2048]{2,1,0:T(8,128)(2,1)} %copy-done.4) | copy-start | bytes 3145732
  185.0 1.2 copy-start.6
  187.6 35.0 %copy-start.3 = (bf16[16,272,128]{2,1,0:T(8,128)(2,1)S(1)}, bf16[16,272,128]{2,1,0:T(8,128)(2,1)}, u32[]{:S(2)}) copy-start(bf16[16,272,128]{2,1,0:T(8,128)(2,1)} %copy-done.2) | copy-start | bytes 3342340
  187.6 35.0 %copy-start.15 = (bf16[16,128,128]{2,1,0:T(8,128)(2,1)S(1)}, bf16[16,128,128]{2,1,0:T(8,128)(2,1)}, u32[]{:S(2)}) copy-start(bf16[16,128,128]{2,1,0:T(8,128)(2,1)} %copy-done.14) | copy-start | bytes 1572868
  188.6 49.5 %collective-permute-start.6 = (bf16[4,128,128]{2,1,0:T(8,128)(2,1)S(1)}, bf16[4,128,128]{2,1,0:T(8,128)(2,1)S(1)}, u32[]{:S(2)}, u32[]{:S(2)}) collective-permute-start(bf16[4,128,128]{2,1,0:T(8,128)(2,1)S(1)} %get-tuple-element.69), channel_id=1, source_target_pairs={{0,1},{1,2},{2,3},{3,0},{4,5},{5,6},{6,7},{7,4},{8,9},{9,10},{10,1... | collective-permute-start | bytes 393224 | tf_op jit(solution)/shard_map/ppermute | solution.py:418
  195.6 42.5 %collective-permute-start.7 = (bf16[4,128,128]{2,1,0:T(8,128)(2,1)S(1)}, bf16[4,128,128]{2,1,0:T(8,128)(2,1)S(1)}, u32[]{:S(2)}, u32[]{:S(2)}) collective-permute-start(bf16[4,128,128]{2,1,0:T(8,128)(2,1)S(1)} %get-tuple-element.70), channel_id=1, source_target_pairs={{0,2},{1,3},{2,0},{3,1},{4,6},{5,7},{6,4},{7,5},{8,10},{9,11},{10,... | collective-permute-start | bytes 393224 | tf_op jit(solution)/shard_map/ppermute | solution.py:418
  202.5 35.6 %collective-permute-start.8 = (bf16[4,128,128]{2,1,0:T(8,128)(2,1)S(1)}, bf16[4,128,128]{2,1,0:T(8,128)(2,1)S(1)}, u32[]{:S(2)}, u32[]{:S(2)}) collective-permute-start(bf16[4,128,128]{2,1,0:T(8,128)(2,1)S(1)} %get-tuple-element.71), channel_id=1, source_target_pairs={{0,3},{1,0},{2,1},{3,2},{4,7},{5,4},{6,5},{7,6},{8,11},{9,8},{10,9... | collective-permute-start | bytes 393224 | tf_op jit(solution)/shard_map/ppermute | solution.py:418
  209.7 28.4 %all-to-all-start.3 = ((bf16[8,432,128]{2,1,0:T(8,128)(2,1)}), bf16[8,432,128]{2,1,0:T(8,128)(2,1)S(1)}, u32[]{:S(2)}, u32[]{:S(2)}) async-start(bf16[8,432,128]{2,1,0:T(8,128)(2,1)} %bitcast.5), calls=%async_computation.3 | async-start | bytes 1769472 | tf_op jit(solution)/shard_map/all_to_all | solution.py:304
  257.7 38.7 %all-to-all-start.4 = ((bf16[16,128,128]{2,1,0:T(8,128)(2,1)}), bf16[16,128,128]{2,1,0:T(8,128)(2,1)S(1)}, u32[]{:S(2)}, u32[]{:S(2)}) async-start(bf16[16,128,128]{2,1,0:T(8,128)(2,1)} %shard_map.112), calls=%async_computation.4 | async-start | bytes 1048576 | tf_op jit(solution)/shard_map/all_to_all | solution.py:304
  261.4 10.1 %collective-permute-start.10 = (bf16[4,128,128]{2,1,0:T(8,128)(2,1)S(1)}, bf16[4,128,128]{2,1,0:T(8,128)(2,1)S(1)}, u32[]{:S(2)}, u32[]{:S(2)}) collective-permute-start(bf16[4,128,128]{2,1,0:T(8,128)(2,1)S(1)} %get-tuple-element.85), channel_id=1, source_target_pairs={{0,8},{1,9},{2,10},{3,11},{4,12},{5,13},{6,14},{7,15},{8,0},{9,1},... | collective-permute-start | bytes 393224 | tf_op jit(solution)/shard_map/ppermute | solution.py:447
  266.1 7.8 %collective-permute-start.11 = (bf16[4,128,128]{2,1,0:T(8,128)(2,1)S(1)}, bf16[4,128,128]{2,1,0:T(8,128)(2,1)S(1)}, u32[]{:S(2)}, u32[]{:S(2)}) collective-permute-start(bf16[4,128,128]{2,1,0:T(8,128)(2,1)S(1)} %get-tuple-element.86), channel_id=1, source_target_pairs={{0,12},{1,13},{2,14},{3,15},{4,0},{5,1},{6,2},{7,3},{8,4},{9,5},{1... | collective-permute-start | bytes 393224 | tf_op jit(solution)/shard_map/ppermute | solution.py:447
  268.9 7.8 %collective-permute-start.9 = (bf16[4,128,128]{2,1,0:T(8,128)(2,1)S(1)}, bf16[4,128,128]{2,1,0:T(8,128)(2,1)S(1)}, u32[]{:S(2)}, u32[]{:S(2)}) collective-permute-start(bf16[4,128,128]{2,1,0:T(8,128)(2,1)S(1)} %get-tuple-element.84), channel_id=1, source_target_pairs={{0,4},{1,5},{2,6},{3,7},{4,8},{5,9},{6,10},{7,11},{8,12},{9,13},{1... | collective-permute-start | bytes 393224 | tf_op jit(solution)/shard_map/ppermute | solution.py:447
Sparse Core Ops, SparseCore 0:
  10.1 51.4 all-gather.12
  63.7 38.3 all-gather.10
  145.3 30.7 all-gather.14

commit v3 on v2

--- a/solution.py
+++ b/solution.py
@@ -159,6 +159,15 @@
         send_ref[d] = joined[d // NZ * PY:(d // NZ + 1) * PY, :]
 
 
+def hold_kernel(a_ref, b_ref, a_out, b_out, sems):
+    first = pltpu.make_async_copy(a_ref, a_out, sems.at[0])
+    second = pltpu.make_async_copy(b_ref, b_out, sems.at[1])
+    first.start()
+    second.start()
+    first.wait()
+    second.wait()
+
+
 def proj1_kernel(r_ref, win_ref, wout_ref, early_ref, preact_ref, send_ref, acc_ref):
     y = pl.program_id(0)
 
@@ -229,20 +238,26 @@
             out_refs[k][y] = jnp.where(low_half((TOK, FEAT)), parts[0], parts[1]).astype(BF)
 
 
-def turn_grad_kernel(a_ref, b_ref, c_ref, d_ref, *out_refs):
-    y = lax.axis_index("seq") // NZ
-    for j in range(NY):
-        for k, ref in enumerate((a_ref, b_ref, c_ref, d_ref)):
-            out_refs[j][k] = ref[(y + j) % NY]
-
-
-def join_grad_kernel(a_ref, b_ref, c_ref, d_ref, out_ref):
+def stack_grad_kernel(a_ref, b_ref, c_ref, d_ref, out_ref):
+    for k, ref in enumerate((a_ref, b_ref, c_ref, d_ref)):
+        out_ref[k] = ref[...]
+
+
+def join_grad_kernel(r_ref, out_ref, held_ref, sems):
     y = lax.axis_index("seq") // NZ
     z = lax.axis_index("seq") % NZ
-    for j, ref in enumerate((a_ref, b_ref, c_ref, d_ref)):
+    copies = []
+    for source in range(NY):
         for k in range(NZ):
-            source = (y + NY - j) % NY * NZ + (z + NZ - k) % NZ
-            out_ref[0, :, pl.ds(pl.multiple_of(source * FEAT, FEAT), FEAT)] = ref[k]
+            n = source * NZ + k
+            copies.append(pltpu.make_async_copy(r_ref.at[source, k, y], held_ref.at[n], sems.at[n]))
+            copies[-1].start()
+    for copy in copies:
+        copy.wait()
+    for source in range(NY):
+        for k in range(NZ):
+            at = pl.multiple_of((source * NZ + (z + NZ - k) % NZ) * FEAT, FEAT)
+            out_ref[0, :, pl.ds(at, FEAT)] = held_ref[source * NZ + k]
 
 
 def bwd_kernel(g_ref, x_ref, v_ref, p_ref, out_ref, d0_ref, d1_ref, w0_ref, w1_ref):
@@ -369,7 +384,16 @@
         out_specs=tuple(whole(3)),
         compiler_params=params(),
     )(pooled_probs, *turned)
+    win, wout, pooled_out = lax.optimization_barrier((win, wout, pooled_out))
     pooled_in = exchange(pooled_out, "seq")
+    win, wout = pl.pallas_call(
+        hold_kernel,
+        out_shape=(sds((NY, WIDTH, FEAT), BF), sds((NY, FEAT, TEACH), BF)),
+        in_specs=[pl.BlockSpec(memory_space=pl.ANY)] * 2,
+        out_specs=tuple(whole(2)),
+        scratch_shapes=[pltpu.SemaphoreType.DMA((2,))],
+        compiler_params=params(1),
+    )(win, wout)
 
     win_spec = pl.BlockSpec((1, WIDTH, FEAT), lambda i: (i, 0, 0))
     wout_spec = pl.BlockSpec((1, FEAT, TEACH), lambda i: (i, 0, 0))
@@ -381,7 +405,7 @@
         in_specs=[fixed((NS, PY, FEAT)), win_spec, wout_spec],
         out_specs=(fixed((PY, EARLY)), slab, fixed((PY, TEACH))),
         scratch_shapes=[pltpu.VMEM((PY, TEACH), F32)],
-        compiler_params=params(59),
+        compiler_params=params(),
     )(pooled_in, win, wout)
     early_in = gather(early, "seq", Y_GROUPS)
     partials = gather(partial, "seq", Z_GROUPS)
@@ -436,23 +460,14 @@
         compiler_params=params(50),
         cost_estimate=pl.CostEstimate(flops=10 ** 10, bytes_accessed=2 * 10 ** 7, transcendentals=0),
     )(grad_rows, x, values, probs)
-    turned = pl.pallas_call(
-        turn_grad_kernel,
-        out_shape=(sds((NZ, TOK, FEAT), BF),) * NY,
+    stacked = pl.pallas_call(
+        stack_grad_kernel,
+        out_shape=sds((NZ, NY, TOK, FEAT), BF),
         in_specs=whole(NZ),
-        out_specs=tuple(whole(NY)),
+        out_specs=whole(1)[0],
         compiler_params=params(),
     )(*moved)
-    turned, grads = lax.optimization_barrier((turned, grads))
-    turned = [turned[0]] + [lax.ppermute(turned[k], "seq", Y_SHIFT[k]) for k in range(1, NY)]
-    grad_value = pl.pallas_call(
-        join_grad_kernel,
-        out_shape=sds((1, TOK, WIDTH), BF),
-        in_specs=whole(NY),
-        out_specs=whole(1)[0],
-        compiler_params=params(),
-    )(*turned)
-    part, grads = lax.optimization_barrier((part, grads))
+    part, grads, stacked = lax.optimization_barrier((part, grads, stacked))
     part = pl.pallas_call(
         sum_kernel,
         out_shape=sds((ROWS_DP, FEAT), BF),
@@ -479,6 +494,15 @@
         compiler_params=params(),
     )(total)
 
+    grad_value = pl.pallas_call(
+        join_grad_kernel,
+        out_shape=sds((1, TOK, WIDTH), BF),
+        in_specs=[pl.BlockSpec(memory_space=pl.ANY)],
+        out_specs=whole(1)[0],
+        scratch_shapes=[pltpu.VMEM((NS, TOK, FEAT), BF), pltpu.SemaphoreType.DMA((NS,))],
+        compiler_params=params(59),
+    )(gather(stacked, "seq", Y_GROUPS))
+    grads_in, grad_value = lax.optimization_barrier((grads_in, grad_value))
     grad_query = pl.pallas_call(
         unpack_kernel,
         grid=(PARTS,),

time: 305 us -> 303 us (level); the launches traced: 304 us -> 298 us
  starting transfers between devices: 115 us -> 106 us
  local copies, waits for them, and re-layouts: 7.43 us -> 13.4 us
    ppermute x3 -> x0, starting transfers between devices: 10.1 us -> none  [per_device(): lax.ppermute(turned[k], 'seq', Y_SHIFT[k])]
    unnamed x34 -> x42, local copies, waits for them, and re-layouts: 7.43 us -> 13.4 us
    ppermute x3 -> x0, waiting for transfers between devices: 5.32 us -> none  [per_device(): lax.ppermute(turned[k], 'seq', Y_SHIFT[k])]
    all_to_all x5, waiting for transfers between devices: 29.6 us -> 33.9 us  [exchange(): lax.all_to_all(array, axis, 0, 0, axis_index_groups=groups, tiled=True)]
  transfers between devices with their start and end apart: 20 -> 18, of which waited for: 9 -> 9; matrix products, arithmetic and copies ran while one was open for 0% -> 0% of each run, Pallas kernels for 14% -> 15%
where the time goes in v3:
time: 303 us; the launch traced here: 298 us
  starting transfers between devices  106 us (35%)
  blocking collectives  61 us (20%)
  waiting for transfers between devices  55.8 us (18%)
  Pallas kernels  47.9 us (16%)
  between operations  14 us (5%)
  local copies, waits for them, and re-layouts  13.4 us (4%)
    all_gather x4, blocking collectives, gather(): lax.all_gather(array, axis, axis=0, axis_index_groups=groups, tiled=False)  61 us
    all_to_all x5, starting transfers between devices, exchange(): lax.all_to_all(array, axis, 0, 0, axis_index_groups=groups, tiled=True)  49.4 us
    all_to_all x5, waiting for transfers between devices, exchange(): lax.all_to_all(array, axis, 0, 0, axis_index_groups=groups, tiled=True)  33.9 us
    ppermute x3, starting transfers between devices, per_device(): lax.ppermute(turned[k], 'seq', Z_SHIFT[k])  25.2 us
    ppermute x3, starting transfers between devices, per_device(): lax.ppermute(moved[k], 'seq', Z_SHIFT[k])  20.8 us
    pallas_call x1, Pallas kernels, per_device(): pl.pallas_call(bwd_kernel, grid=(LEN // BBLK,), out_shape=sds((NS, TOK, F...  15.5 us
    pallas_call x1, Pallas kernels, per_device(): pl.pallas_call(fwd_kernel, grid=(LEN // FBLK,), out_shape=(sds((2, LEN, L...  14.5 us
    unnamed x42, local copies, waits for them, and re-layouts  13.4 us
  transfers between devices with their start and end apart: 18, of which 9 were waited for; matrix products, arithmetic and copies ran while one was open for 0% of the time, Pallas kernels for 15%

profile of v3, /device:TPU:1, one launch (start us, length us, event | category | flops | bytes accessed | tf_op | source)
XLA Modules:
  0.0 298.3 jit_solution(5593605399158061272)
XLA Ops:
  7.2 0.7 all-gather.15.cloned.1.call-update
  7.9 3.5 %shard_map.102 = bf16[16,272,128]{2,1,0:T(8,128)(2,1)} custom-call(bf16[1,128,2048]{2,1,0:T(8,128)(2,1)} %q_ref.1, bf16[1,128,2048]{2,1,0:T(8,128)(2,1)} %k_ref.1, s32[1,128]{1,0:T(1,128)} %ids_ref.1), custom_call_target="tpu_custom_call" | custom-call | tf_op jit(solution)/shard_map/pallas_call | solution.py:336
  11.4 18.5 %all-to-all-start = ((bf16[16,272,128]{2,1,0:T(8,128)(2,1)}), bf16[16,272,128]{2,1,0:T(8,128)(2,1)S(1)}, u32[]{:S(2)}, u32[]{:S(2)}) async-start(bf16[16,272,128]{2,1,0:T(8,128)(2,1)} %shard_map.102), calls=%async_computation | async-start | bytes 2228224 | tf_op jit(solution)/shard_map/all_to_all | solution.py:319
  30.0 0.7 all-gather.13.cloned.1.call-update
  30.8 3.3 %collective-permute-start = (bf16[4,128,128]{2,1,0:T(8,128)(2,1)S(1)}, bf16[4,128,128]{2,1,0:T(8,128)(2,1)S(1)}, u32[]{:S(2)}, u32[]{:S(2)}) collective-permute-start(bf16[4,128,128]{2,1,0:T(8,128)(2,1)S(1)} %get-tuple-element.50), channel_id=1, source_target_pairs={{0,4},{1,5},{2,6},{3,7},{4,8},{5,9},{6,10},{7,11},{8,12},{9,13},{1... | collective-permute-start | bytes 393224 | tf_op jit(solution)/shard_map/ppermute | solution.py:353
  34.1 4.3 %collective-permute-start.1 = (bf16[4,128,128]{2,1,0:T(8,128)(2,1)S(1)}, bf16[4,128,128]{2,1,0:T(8,128)(2,1)S(1)}, u32[]{:S(2)}, u32[]{:S(2)}) collective-permute-start(bf16[4,128,128]{2,1,0:T(8,128)(2,1)S(1)} %get-tuple-element.51), channel_id=1, source_target_pairs={{0,8},{1,9},{2,10},{3,11},{4,12},{5,13},{6,14},{7,15},{8,0},{9,1},... | collective-permute-start | bytes 393224 | tf_op jit(solution)/shard_map/ppermute | solution.py:353
  38.4 3.1 %collective-permute-start.2 = (bf16[4,128,128]{2,1,0:T(8,128)(2,1)S(1)}, bf16[4,128,128]{2,1,0:T(8,128)(2,1)S(1)}, u32[]{:S(2)}, u32[]{:S(2)}) collective-permute-start(bf16[4,128,128]{2,1,0:T(8,128)(2,1)S(1)} %get-tuple-element.52), channel_id=1, source_target_pairs={{0,12},{1,13},{2,14},{3,15},{4,0},{5,1},{6,2},{7,3},{8,4},{9,5},{1... | collective-permute-start | bytes 393224 | tf_op jit(solution)/shard_map/ppermute | solution.py:353
  41.5 2.0 collective-permute-done.b_ref
  43.6 9.5 %collective-permute-done.1.c_ref = bf16[4,128,128]{2,1,0:T(8,128)(2,1)S(1)} collective-permute-done((bf16[4,128,128]{2,1,0:T(8,128)(2,1)S(1)}, bf16[4,128,128]{2,1,0:T(8,128)(2,1)S(1)}, u32[]{:S(2)}, u32[]{:S(2)}) %collective-permute-start.1) | collective-permute-done | bytes 131104 | tf_op jit(solution)/shard_map/ppermute | solution.py:353
  53.1 1.6 collective-permute-done.2.d_ref
  54.7 7.9 %collective-permute-start.3 = (bf16[608,128]{1,0:T(8,128)(2,1)S(1)}, bf16[608,128]{1,0:T(8,128)(2,1)S(1)}, u32[]{:S(2)}, u32[]{:S(2)}) collective-permute-start(bf16[608,128]{1,0:T(8,128)(2,1)S(1)} %get-tuple-element.55), channel_id=1, source_target_pairs={{0,1},{1,2},{2,3},{3,0},{4,5},{5,6},{6,7},{7,4},{8,9},{9,10},{10,1... | collective-permute-start | bytes 466952 | tf_op jit(solution)/shard_map/ppermute | solution.py:361
  62.7 10.0 %collective-permute-start.4 = (bf16[608,128]{1,0:T(8,128)(2,1)S(1)}, bf16[608,128]{1,0:T(8,128)(2,1)S(1)}, u32[]{:S(2)}, u32[]{:S(2)}) collective-permute-start(bf16[608,128]{1,0:T(8,128)(2,1)S(1)} %get-tuple-element.56), channel_id=1, source_target_pairs={{0,2},{1,3},{2,0},{3,1},{4,6},{5,7},{6,4},{7,5},{8,10},{9,11},{10,... | collective-permute-start | bytes 466952 | tf_op jit(solution)/shard_map/ppermute | solution.py:361
  72.7 7.3 %collective-permute-start.5 = (bf16[608,128]{1,0:T(8,128)(2,1)S(1)}, bf16[608,128]{1,0:T(8,128)(2,1)S(1)}, u32[]{:S(2)}, u32[]{:S(2)}) collective-permute-start(bf16[608,128]{1,0:T(8,128)(2,1)S(1)} %get-tuple-element.57), channel_id=1, source_target_pairs={{0,3},{1,0},{2,1},{3,2},{4,7},{5,4},{6,5},{7,6},{8,11},{9,8},{10,9... | collective-permute-start | bytes 466952 | tf_op jit(solution)/shard_map/ppermute | solution.py:361
  80.0 13.6 %all-to-all-done.x_ref = bf16[16,272,128]{2,1,0:T(8,128)(2,1)S(1)} async-done(((bf16[16,272,128]{2,1,0:T(8,128)(2,1)}), bf16[16,272,128]{2,1,0:T(8,128)(2,1)S(1)}, u32[]{:S(2)}, u32[]{:S(2)}) %all-to-all-start) | async-done | bytes 1114144 | tf_op jit(solution)/shard_map/all_to_all | solution.py:319
  93.6 14.5 %shard_map.103 = (bf16[2,2048,2048]{2,1,0:T(8,128)(2,1)}, bf16[2,128,2048]{2,1,0:T(8,128)(2,1)S(1)}) custom-call(bf16[16,272,128]{2,1,0:T(8,128)(2,1)S(1)} %all-to-all-done.x_ref), custom_call_target="tpu_custom_call" | custom-call | flops 1000000 | bytes 1000000 | tf_op jit(solution)/shard_map/pallas_call | solution.py:363
  108.1 6.6 %collective-permute-done.4.c_ref = bf16[608,128]{1,0:T(8,128)(2,1)S(1)} collective-permute-done((bf16[608,128]{1,0:T(8,128)(2,1)S(1)}, bf16[608,128]{1,0:T(8,128)(2,1)S(1)}, u32[]{:S(2)}, u32[]{:S(2)}) %collective-permute-start.4) | collective-permute-done | bytes 155680 | tf_op jit(solution)/shard_map/ppermute | solution.py:361
  114.7 1.2 shard_map.106
  115.8 1.0 copy-done.2
  117.5 0.8 copy-done.17
  118.3 5.9 %all-to-all-start.1 = ((bf16[16,32,128]{2,1,0:T(8,128)(2,1)}), bf16[16,32,128]{2,1,0:T(8,128)(2,1)}, u32[]{:S(2)}, u32[]{:S(2)}) async-start(bf16[16,32,128]{2,1,0:T(8,128)(2,1)} %get-tuple-element.59), calls=%async_computation.1 | async-start | bytes 262144 | tf_op jit(solution)/shard_map/all_to_all | solution.py:319
  124.2 1.6 copy-done.4
  125.8 1.4 copy-done.5
  127.6 11.9 %all-to-all-done.1.r_ref = bf16[16,32,128]{2,1,0:T(8,128)(2,1)} async-done(((bf16[16,32,128]{2,1,0:T(8,128)(2,1)}), bf16[16,32,128]{2,1,0:T(8,128)(2,1)}, u32[]{:S(2)}, u32[]{:S(2)}) %all-to-all-start.1) | async-done | bytes 131104 | tf_op jit(solution)/shard_map/all_to_all | solution.py:319
  139.5 2.5 shard_map.108
  142.0 0.7 copy-done.8
  144.0 15.8 %all-gather.3 = bf16[128,1408]{1,0:T(8,128)(2,1)S(1)} all-gather(bf16[32,1408]{1,0:T(8,128)(2,1)} %copy-done.13), channel_id=5, replica_groups={{0,1,2,3},{4,5,6,7},{8,9,10,11},{12,13,14,15},{16,17,18,19},{20,21,22,2..., dimensions={0}, use_global_device_ids=true | all-gather | bytes 450560 | tf_op jit(solution)/shard_map/all_gather | solution.py:323
  159.8 0.9 copy-done.10
  160.7 0.8 copy-done.15
  161.6 2.6 shard_map.109
  165.5 7.4 %all-to-all-start.2 = ((bf16[16,32,128]{2,1,0:T(8,128)(2,1)}), bf16[16,32,128]{2,1,0:T(8,128)(2,1)S(1)}, u32[]{:S(2)}, u32[]{:S(2)}) async-start(bf16[16,32,128]{2,1,0:T(8,128)(2,1)} %copy-done.11), calls=%async_computation.2 | async-start | bytes 262144 | tf_op jit(solution)/shard_map/all_to_all | solution.py:319
  172.9 11.1 %all-gather.4 = bf16[128,1920]{1,0:T(8,128)(2,1)S(1)} all-gather(bf16[32,1920]{1,0:T(8,128)(2,1)} %copy-done.12), channel_id=6, replica_groups={{0,4,8,12},{1,5,9,13},{2,6,10,14},{3,7,11,15},{16,20,24,28},{17,21,25,2..., dimensions={0}, use_global_device_ids=true | all-gather | bytes 614400 | tf_op jit(solution)/shard_map/all_gather | solution.py:323
  184.0 1.2 copy-done.6
  185.2 1.4 shard_map.110
  188.4 12.7 %all-to-all-start.3 = ((bf16[8,432,128]{2,1,0:T(8,128)(2,1)}), bf16[8,432,128]{2,1,0:T(8,128)(2,1)S(1)}, u32[]{:S(2)}, u32[]{:S(2)}) async-start(bf16[8,432,128]{2,1,0:T(8,128)(2,1)} %bitcast.5), calls=%async_computation.3 | async-start | bytes 1769472 | tf_op jit(solution)/shard_map/all_to_all | solution.py:319
  201.1 6.9 %collective-permute-start.6 = (bf16[4,128,128]{2,1,0:T(8,128)(2,1)S(1)}, bf16[4,128,128]{2,1,0:T(8,128)(2,1)S(1)}, u32[]{:S(2)}, u32[]{:S(2)}) collective-permute-start(bf16[4,128,128]{2,1,0:T(8,128)(2,1)S(1)} %copy-done.20), channel_id=1, source_target_pairs={{0,1},{1,2},{2,3},{3,0},{4,5},{5,6},{6,7},{7,4},{8,9},{9,10},{10,1... | collective-permute-start | bytes 393224 | tf_op jit(solution)/shard_map/ppermute | solution.py:442
  208.0 7.1 %collective-permute-start.7 = (bf16[4,128,128]{2,1,0:T(8,128)(2,1)S(1)}, bf16[4,128,128]{2,1,0:T(8,128)(2,1)S(1)}, u32[]{:S(2)}, u32[]{:S(2)}) collective-permute-start(bf16[4,128,128]{2,1,0:T(8,128)(2,1)S(1)} %get-tuple-element.77), channel_id=1, source_target_pairs={{0,2},{1,3},{2,0},{3,1},{4,6},{5,7},{6,4},{7,5},{8,10},{9,11},{10,... | collective-permute-start | bytes 393224 | tf_op jit(solution)/shard_map/ppermute | solution.py:442
  215.2 6.8 %collective-permute-start.8 = (bf16[4,128,128]{2,1,0:T(8,128)(2,1)S(1)}, bf16[4,128,128]{2,1,0:T(8,128)(2,1)S(1)}, u32[]{:S(2)}, u32[]{:S(2)}) collective-permute-start(bf16[4,128,128]{2,1,0:T(8,128)(2,1)S(1)} %get-tuple-element.78), channel_id=1, source_target_pairs={{0,3},{1,0},{2,1},{3,2},{4,7},{5,4},{6,5},{7,6},{8,11},{9,8},{10,9... | collective-permute-start | bytes 393224 | tf_op jit(solution)/shard_map/ppermute | solution.py:442
  222.0 1.0 copy-done.18
  223.0 15.5 %shard_map.112 = bf16[16,128,128]{2,1,0:T(8,128)(2,1)} custom-call(bf16[128,128]{1,0:T(8,128)(2,1)S(1)} %get-tuple-element.72.g_ref, bf16[16,272,128]{2,1,0:T(8,128)(2,1)S(1)} %copy-done.1, bf16[16,128,128]{2,1,0:T(8,128)(2,1)S(1)} %copy-done.18, bf16[2,2048,2048]{2,1,0:T(8,128)(2,1)} %get-tuple-element.74.p_ref), custom_call_target="tpu_custom_call" | custom-call | flops 10000000000 | bytes 20000000 | tf_op jit(solution)/shard_map/pallas_call | solution.py:443
  238.5 0.8 shard_map.113
  239.5 17.9 %all-gather.5 = bf16[1728,128]{1,0:T(8,128)(2,1)S(1)} all-gather(bf16[432,128]{1,0:T(8,128)(2,1)S(1)} %shard_map.114), channel_id=7, replica_groups={{0,32,64,96},{16,48,80,112},{128,160,192,224},{144,176,208,240},{256,28..., dimensions={0}, use_global_device_ids=true | all-gather | bytes 552960 | tf_op jit(solution)/shard_map/all_gather | solution.py:323
  257.4 4.9 %all-to-all-start.4 = ((bf16[16,128,128]{2,1,0:T(8,128)(2,1)}), bf16[16,128,128]{2,1,0:T(8,128)(2,1)S(1)}, u32[]{:S(2)}, u32[]{:S(2)}) async-start(bf16[16,128,128]{2,1,0:T(8,128)(2,1)} %shard_map.112), calls=%async_computation.4 | async-start | bytes 1048576 | tf_op jit(solution)/shard_map/all_to_all | solution.py:319
  262.3 16.2 %all-gather.7.r_ref = bf16[3456,128]{1,0:T(8,128)(2,1)S(1)} all-gather(bf16[432,128]{1,0:T(8,128)(2,1)S(1)} %shard_map.117), channel_id=9, replica_groups={{0,16,128,144,256,272,384,400},{32,48,160,176,288,304,416,432},{64,80,1..., dimensions={0}, use_global_device_ids=true | all-gather | bytes 995328 | tf_op jit(solution)/shard_map/all_gather | solution.py:323
  278.5 1.3 shard_map.118
  279.8 0.8 all-gather.19.cloned.1.call-done
  280.6 2.1 shard_map.115
  282.6 7.8 %all-to-all-done.4.r_ref = bf16[16,128,128]{2,1,0:T(8,128)(2,1)S(1)} async-done(((bf16[16,128,128]{2,1,0:T(8,128)(2,1)}), bf16[16,128,128]{2,1,0:T(8,128)(2,1)S(1)}, u32[]{:S(2)}, u32[]{:S(2)}) %all-to-all-start.4) | async-done | bytes 524320 | tf_op jit(solution)/shard_map/all_to_all | solution.py:319
  290.4 1.4 shard_map.116
  (55 shorter events, 6.0 us)
Async XLA Ops:
  7.2 111.1 %all-gather.15.cloned.1.call-start = ((), (), s32[]{:S(2)}) async-start(), calls=%async_computation.6 | async-start | bytes 1802240 | tf_op jit(solution)/shard_map/all_gather | solution.py:323
  11.4 19.3 %copy-start.7 = (bf16[1,128,2048]{2,1,0:T(8,128)(2,1)S(1)}, bf16[1,128,2048]{2,1,0:T(8,128)(2,1)}, u32[]{:S(2)}) copy-start(bf16[1,128,2048]{2,1,0:T(8,128)(2,1)} %v_ref) | copy-start | bytes 1572868
  11.4 43.3 %copy-start.16 = (bf16[1,8,1408]{2,1,0:T(8,128)(2,1)S(1)}, bf16[1,8,1408]{2,1,0:T(8,128)(2,1)}, u32[]{:S(2)}) copy-start(bf16[1,8,1408]{2,1,0:T(8,128)(2,1)} %teacher_ref) | copy-start | bytes 67588
  11.4 82.2 %all-to-all-start = ((bf16[16,272,128]{2,1,0:T(8,128)(2,1)}), bf16[16,272,128]{2,1,0:T(8,128)(2,1)S(1)}, u32[]{:S(2)}, u32[]{:S(2)}) async-start(bf16[16,272,128]{2,1,0:T(8,128)(2,1)} %shard_map.102), calls=%async_computation | async-start | bytes 2228224 | tf_op jit(solution)/shard_map/all_to_all | solution.py:319
  29.9 88.3 %all-gather.13.cloned.1.call-start = ((), (), s32[]{:S(2)}) async-start(), calls=%async_computation.5 | async-start | bytes 2621440 | tf_op jit(solution)/shard_map/all_gather | solution.py:323
  30.8 12.7 %collective-permute-start = (bf16[4,128,128]{2,1,0:T(8,128)(2,1)S(1)}, bf16[4,128,128]{2,1,0:T(8,128)(2,1)S(1)}, u32[]{:S(2)}, u32[]{:S(2)}) collective-permute-start(bf16[4,128,128]{2,1,0:T(8,128)(2,1)S(1)} %get-tuple-element.50), channel_id=1, source_target_pairs={{0,4},{1,5},{2,6},{3,7},{4,8},{5,9},{6,10},{7,11},{8,12},{9,13},{1... | collective-permute-start | bytes 393224 | tf_op jit(solution)/shard_map/ppermute | solution.py:353
  34.1 18.9 %collective-permute-start.1 = (bf16[4,128,128]{2,1,0:T(8,128)(2,1)S(1)}, bf16[4,128,128]{2,1,0:T(8,128)(2,1)S(1)}, u32[]{:S(2)}, u32[]{:S(2)}) collective-permute-start(bf16[4,128,128]{2,1,0:T(8,128)(2,1)S(1)} %get-tuple-element.51), channel_id=1, source_target_pairs={{0,8},{1,9},{2,10},{3,11},{4,12},{5,13},{6,14},{7,15},{8,0},{9,1},... | collective-permute-start | bytes 393224 | tf_op jit(solution)/shard_map/ppermute | solution.py:353
  38.4 16.2 %collective-permute-start.2 = (bf16[4,128,128]{2,1,0:T(8,128)(2,1)S(1)}, bf16[4,128,128]{2,1,0:T(8,128)(2,1)S(1)}, u32[]{:S(2)}, u32[]{:S(2)}) collective-permute-start(bf16[4,128,128]{2,1,0:T(8,128)(2,1)S(1)} %get-tuple-element.52), channel_id=1, source_target_pairs={{0,12},{1,13},{2,14},{3,15},{4,0},{5,1},{6,2},{7,3},{8,4},{9,5},{1... | collective-permute-start | bytes 393224 | tf_op jit(solution)/shard_map/ppermute | solution.py:353
  54.7 53.3 %collective-permute-start.3 = (bf16[608,128]{1,0:T(8,128)(2,1)S(1)}, bf16[608,128]{1,0:T(8,128)(2,1)S(1)}, u32[]{:S(2)}, u32[]{:S(2)}) collective-permute-start(bf16[608,128]{1,0:T(8,128)(2,1)S(1)} %get-tuple-element.55), channel_id=1, source_target_pairs={{0,1},{1,2},{2,3},{3,0},{4,5},{5,6},{6,7},{7,4},{8,9},{9,10},{10,1... | collective-permute-start | bytes 466952 | tf_op jit(solution)/shard_map/ppermute | solution.py:361
  62.7 52.0 %collective-permute-start.4 = (bf16[608,128]{1,0:T(8,128)(2,1)S(1)}, bf16[608,128]{1,0:T(8,128)(2,1)S(1)}, u32[]{:S(2)}, u32[]{:S(2)}) collective-permute-start(bf16[608,128]{1,0:T(8,128)(2,1)S(1)} %get-tuple-element.56), channel_id=1, source_target_pairs={{0,2},{1,3},{2,0},{3,1},{4,6},{5,7},{6,4},{7,5},{8,10},{9,11},{10,... | collective-permute-start | bytes 466952 | tf_op jit(solution)/shard_map/ppermute | solution.py:361
  72.7 42.0 %collective-permute-start.5 = (bf16[608,128]{1,0:T(8,128)(2,1)S(1)}, bf16[608,128]{1,0:T(8,128)(2,1)S(1)}, u32[]{:S(2)}, u32[]{:S(2)}) collective-permute-start(bf16[608,128]{1,0:T(8,128)(2,1)S(1)} %get-tuple-element.57), channel_id=1, source_target_pairs={{0,3},{1,0},{2,1},{3,2},{4,7},{5,4},{6,5},{7,6},{8,11},{9,8},{10,9... | collective-permute-start | bytes 466952 | tf_op jit(solution)/shard_map/ppermute | solution.py:361
  93.6 24.7 %copy-start = (bf16[16,272,128]{2,1,0:T(8,128)(2,1)}, bf16[16,272,128]{2,1,0:T(8,128)(2,1)S(1)}, u32[]{:S(2)}) copy-start(bf16[16,272,128]{2,1,0:T(8,128)(2,1)S(1)} %all-to-all-done.x_ref) | copy-start | bytes 3342340
  115.8 1.0 copy-start.2
  116.8 0.7 copy-start.9
  117.5 0.8 copy-start.17
  118.3 21.2 %all-to-all-start.1 = ((bf16[16,32,128]{2,1,0:T(8,128)(2,1)}), bf16[16,32,128]{2,1,0:T(8,128)(2,1)}, u32[]{:S(2)}, u32[]{:S(2)}) async-start(bf16[16,32,128]{2,1,0:T(8,128)(2,1)} %get-tuple-element.59), calls=%async_computation.1 | async-start | bytes 262144 | tf_op jit(solution)/shard_map/all_to_all | solution.py:319
  124.2 59.8 %all-gather.17.cloned.1.call-start = ((), (), s32[]{:S(2)}) async-start(), calls=%async_computation.7 | async-start | bytes 1351680 | tf_op jit(solution)/shard_map/all_gather | solution.py:323
  124.2 1.6 copy-start.4
  125.8 1.4 copy-start.5
  142.0 0.7 copy-start.8
  142.7 0.6 copy-start.13
  143.4 0.6 copy-start.14
  159.8 0.9 copy-start.10
  160.7 0.8 copy-start.15
  164.2 0.7 copy-start.11
  164.8 0.7 copy-start.12
  165.5 21.7 %all-to-all-start.2 = ((bf16[16,32,128]{2,1,0:T(8,128)(2,1)}), bf16[16,32,128]{2,1,0:T(8,128)(2,1)S(1)}, u32[]{:S(2)}, u32[]{:S(2)}) async-start(bf16[16,32,128]{2,1,0:T(8,128)(2,1)} %copy-done.11), calls=%async_computation.2 | async-start | bytes 262144 | tf_op jit(solution)/shard_map/all_to_all | solution.py:319
  172.9 14.3 %copy-start.3 = (bf16[2,128,2048]{2,1,0:T(8,128)(2,1)S(1)}, bf16[2,128,2048]{2,1,0:T(8,128)(2,1)}, u32[]{:S(2)}) copy-start(bf16[2,128,2048]{2,1,0:T(8,128)(2,1)} %copy-done.2) | copy-start | bytes 3145732
  184.0 1.2 copy-start.6
  186.6 35.4 %copy-start.1 = (bf16[16,272,128]{2,1,0:T(8,128)(2,1)S(1)}, bf16[16,272,128]{2,1,0:T(8,128)(2,1)}, u32[]{:S(2)}) copy-start(bf16[16,272,128]{2,1,0:T(8,128)(2,1)} %copy-done) | copy-start | bytes 3342340
  187.7 0.7 copy-start.19
  188.4 12.7 %copy-start.20 = (bf16[4,128,128]{2,1,0:T(8,128)(2,1)S(1)}, bf16[4,128,128]{2,1,0:T(8,128)(2,1)}, u32[]{:S(2)}) copy-start(bf16[4,128,128]{2,1,0:T(8,128)(2,1)} %copy-done.19) | copy-start | bytes 393220
  188.4 51.0 %all-to-all-start.3 = ((bf16[8,432,128]{2,1,0:T(8,128)(2,1)}), bf16[8,432,128]{2,1,0:T(8,128)(2,1)S(1)}, u32[]{:S(2)}, u32[]{:S(2)}) async-start(bf16[8,432,128]{2,1,0:T(8,128)(2,1)} %bitcast.5), calls=%async_computation.3 | async-start | bytes 1769472 | tf_op jit(solution)/shard_map/all_to_all | solution.py:319
  201.1 79.5 %all-gather.19.cloned.1.call-start = ((), (), s32[]{:S(2)}) async-start(), calls=%async_computation.8 | async-start | bytes 2621440 | tf_op jit(solution)/shard_map/all_gather | solution.py:323
  201.1 37.4 %collective-permute-start.6 = (bf16[4,128,128]{2,1,0:T(8,128)(2,1)S(1)}, bf16[4,128,128]{2,1,0:T(8,128)(2,1)S(1)}, u32[]{:S(2)}, u32[]{:S(2)}) collective-permute-start(bf16[4,128,128]{2,1,0:T(8,128)(2,1)S(1)} %copy-done.20), channel_id=1, source_target_pairs={{0,1},{1,2},{2,3},{3,0},{4,5},{5,6},{6,7},{7,4},{8,9},{9,10},{10,1... | collective-permute-start | bytes 393224 | tf_op jit(solution)/shard_map/ppermute | solution.py:442
  208.0 30.5 %collective-permute-start.7 = (bf16[4,128,128]{2,1,0:T(8,128)(2,1)S(1)}, bf16[4,128,128]{2,1,0:T(8,128)(2,1)S(1)}, u32[]{:S(2)}, u32[]{:S(2)}) collective-permute-start(bf16[4,128,128]{2,1,0:T(8,128)(2,1)S(1)} %get-tuple-element.77), channel_id=1, source_target_pairs={{0,2},{1,3},{2,0},{3,1},{4,6},{5,7},{6,4},{7,5},{8,10},{9,11},{10,... | collective-permute-start | bytes 393224 | tf_op jit(solution)/shard_map/ppermute | solution.py:442
  215.2 23.4 %collective-permute-start.8 = (bf16[4,128,128]{2,1,0:T(8,128)(2,1)S(1)}, bf16[4,128,128]{2,1,0:T(8,128)(2,1)S(1)}, u32[]{:S(2)}, u32[]{:S(2)}) collective-permute-start(bf16[4,128,128]{2,1,0:T(8,128)(2,1)S(1)} %get-tuple-element.78), channel_id=1, source_target_pairs={{0,3},{1,0},{2,1},{3,2},{4,7},{5,4},{6,5},{7,6},{8,11},{9,8},{10,9... | collective-permute-start | bytes 393224 | tf_op jit(solution)/shard_map/ppermute | solution.py:442
  222.0 1.0 copy-start.18
  257.4 33.0 %all-to-all-start.4 = ((bf16[16,128,128]{2,1,0:T(8,128)(2,1)}), bf16[16,128,128]{2,1,0:T(8,128)(2,1)S(1)}, u32[]{:S(2)}, u32[]{:S(2)}) async-start(bf16[16,128,128]{2,1,0:T(8,128)(2,1)} %shard_map.112), calls=%async_computation.4 | async-start | bytes 1048576 | tf_op jit(solution)/shard_map/all_to_all | solution.py:319
Sparse Core Ops, SparseCore 0:
  10.1 51.5 all-gather.14
  63.7 38.3 all-gather.12
  144.1 31.2 all-gather.16
  239.5 41.0 all-gather.18

commit v4 on v3

--- a/solution.py
+++ b/solution.py
@@ -29,7 +29,7 @@
 FBLK = 512
 BBLK = 256
 CHUNK = 16
-PARTS = 4
+PARTS = 2
 MIB = 1024 * 1024
 
 Y_GROUPS = [[y * 4 + z for y in range(4)] for z in range(4)]

time: 303 us -> 302 us (level)
  transfers between devices with their start and end apart: 18 -> 18, of which waited for: 9 -> 7; matrix products, arithmetic and copies ran while one was open for 0% -> 0% of each run, Pallas kernels for 15% -> 14%
where the time goes in v4:
time: 302 us; the launch traced here: 298 us
  starting transfers between devices  106 us (35%)
  blocking collectives  63.8 us (21%)
  waiting for transfers between devices  54.7 us (18%)
  Pallas kernels  46.1 us (15%)
  between operations  14 us (5%)
  local copies, waits for them, and re-layouts  13.4 us (4%)
    all_gather x4, blocking collectives, gather(): lax.all_gather(array, axis, axis=0, axis_index_groups=groups, tiled=False)  63.8 us
    all_to_all x5, starting transfers between devices, exchange(): lax.all_to_all(array, axis, 0, 0, axis_index_groups=groups, tiled=True)  50.9 us
    all_to_all x5, waiting for transfers between devices, exchange(): lax.all_to_all(array, axis, 0, 0, axis_index_groups=groups, tiled=True)  32.7 us
    ppermute x3, starting transfers between devices, per_device(): lax.ppermute(turned[k], 'seq', Z_SHIFT[k])  23 us
    ppermute x3, starting transfers between devices, per_device(): lax.ppermute(moved[k], 'seq', Z_SHIFT[k])  20.9 us
    pallas_call x1, Pallas kernels, per_device(): pl.pallas_call(bwd_kernel, grid=(LEN // BBLK,), out_shape=sds((NS, TOK, F...  15.5 us
    pallas_call x1, Pallas kernels, per_device(): pl.pallas_call(fwd_kernel, grid=(LEN // FBLK,), out_shape=(sds((2, LEN, L...  14.5 us
    ppermute x3, waiting for transfers between devices, per_device(): lax.ppermute(pieces[k], 'seq', Y_SHIFT[k])  14 us
  transfers between devices with their start and end apart: 18, of which 7 were waited for; matrix products, arithmetic and copies ran while one was open for 0% of the time, Pallas kernels for 14%

profile of v4, /device:TPU:1, one launch (start us, length us, event | category | flops | bytes accessed | tf_op | source)
XLA Modules:
  0.0 297.5 jit_solution(9897776553335264283)
XLA Ops:
  7.2 0.7 all-gather.15.cloned.1.call-update
  7.9 2.2 shard_map.102
  10.1 18.5 %all-to-all-start = ((bf16[16,272,128]{2,1,0:T(8,128)(2,1)}), bf16[16,272,128]{2,1,0:T(8,128)(2,1)S(1)}, u32[]{:S(2)}, u32[]{:S(2)}) async-start(bf16[16,272,128]{2,1,0:T(8,128)(2,1)} %shard_map.102), calls=%async_computation | async-start | bytes 2228224 | tf_op jit(solution)/shard_map/all_to_all | solution.py:319
  28.7 0.7 all-gather.13.cloned.1.call-update
  29.5 3.3 %collective-permute-start = (bf16[4,128,128]{2,1,0:T(8,128)(2,1)S(1)}, bf16[4,128,128]{2,1,0:T(8,128)(2,1)S(1)}, u32[]{:S(2)}, u32[]{:S(2)}) collective-permute-start(bf16[4,128,128]{2,1,0:T(8,128)(2,1)S(1)} %get-tuple-element.50), channel_id=1, source_target_pairs={{0,4},{1,5},{2,6},{3,7},{4,8},{5,9},{6,10},{7,11},{8,12},{9,13},{1... | collective-permute-start | bytes 393224 | tf_op jit(solution)/shard_map/ppermute | solution.py:353
  32.8 4.3 %collective-permute-start.1 = (bf16[4,128,128]{2,1,0:T(8,128)(2,1)S(1)}, bf16[4,128,128]{2,1,0:T(8,128)(2,1)S(1)}, u32[]{:S(2)}, u32[]{:S(2)}) collective-permute-start(bf16[4,128,128]{2,1,0:T(8,128)(2,1)S(1)} %get-tuple-element.51), channel_id=1, source_target_pairs={{0,8},{1,9},{2,10},{3,11},{4,12},{5,13},{6,14},{7,15},{8,0},{9,1},... | collective-permute-start | bytes 393224 | tf_op jit(solution)/shard_map/ppermute | solution.py:353
  37.1 3.1 %collective-permute-start.2 = (bf16[4,128,128]{2,1,0:T(8,128)(2,1)S(1)}, bf16[4,128,128]{2,1,0:T(8,128)(2,1)S(1)}, u32[]{:S(2)}, u32[]{:S(2)}) collective-permute-start(bf16[4,128,128]{2,1,0:T(8,128)(2,1)S(1)} %get-tuple-element.52), channel_id=1, source_target_pairs={{0,12},{1,13},{2,14},{3,15},{4,0},{5,1},{6,2},{7,3},{8,4},{9,5},{1... | collective-permute-start | bytes 393224 | tf_op jit(solution)/shard_map/ppermute | solution.py:353
  40.2 9.1 %collective-permute-done.1.c_ref = bf16[4,128,128]{2,1,0:T(8,128)(2,1)S(1)} collective-permute-done((bf16[4,128,128]{2,1,0:T(8,128)(2,1)S(1)}, bf16[4,128,128]{2,1,0:T(8,128)(2,1)S(1)}, u32[]{:S(2)}, u32[]{:S(2)}) %collective-permute-start.1) | collective-permute-done | bytes 131104 | tf_op jit(solution)/shard_map/ppermute | solution.py:353
  49.4 4.9 %collective-permute-done.2.d_ref = bf16[4,128,128]{2,1,0:T(8,128)(2,1)S(1)} collective-permute-done((bf16[4,128,128]{2,1,0:T(8,128)(2,1)S(1)}, bf16[4,128,128]{2,1,0:T(8,128)(2,1)S(1)}, u32[]{:S(2)}, u32[]{:S(2)}) %collective-permute-start.2) | collective-permute-done | bytes 131104 | tf_op jit(solution)/shard_map/ppermute | solution.py:353
  54.3 7.0 %collective-permute-start.3 = (bf16[608,128]{1,0:T(8,128)(2,1)S(1)}, bf16[608,128]{1,0:T(8,128)(2,1)S(1)}, u32[]{:S(2)}, u32[]{:S(2)}) collective-permute-start(bf16[608,128]{1,0:T(8,128)(2,1)S(1)} %get-tuple-element.55), channel_id=1, source_target_pairs={{0,1},{1,2},{2,3},{3,0},{4,5},{5,6},{6,7},{7,4},{8,9},{9,10},{10,1... | collective-permute-start | bytes 466952 | tf_op jit(solution)/shard_map/ppermute | solution.py:361
  61.3 8.8 %collective-permute-start.4 = (bf16[608,128]{1,0:T(8,128)(2,1)S(1)}, bf16[608,128]{1,0:T(8,128)(2,1)S(1)}, u32[]{:S(2)}, u32[]{:S(2)}) collective-permute-start(bf16[608,128]{1,0:T(8,128)(2,1)S(1)} %get-tuple-element.56), channel_id=1, source_target_pairs={{0,2},{1,3},{2,0},{3,1},{4,6},{5,7},{6,4},{7,5},{8,10},{9,11},{10,... | collective-permute-start | bytes 466952 | tf_op jit(solution)/shard_map/ppermute | solution.py:361
  70.1 7.3 %collective-permute-start.5 = (bf16[608,128]{1,0:T(8,128)(2,1)S(1)}, bf16[608,128]{1,0:T(8,128)(2,1)S(1)}, u32[]{:S(2)}, u32[]{:S(2)}) collective-permute-start(bf16[608,128]{1,0:T(8,128)(2,1)S(1)} %get-tuple-element.57), channel_id=1, source_target_pairs={{0,3},{1,0},{2,1},{3,2},{4,7},{5,4},{6,5},{7,6},{8,11},{9,8},{10,9... | collective-permute-start | bytes 466952 | tf_op jit(solution)/shard_map/ppermute | solution.py:361
  77.3 14.9 %all-to-all-done.x_ref = bf16[16,272,128]{2,1,0:T(8,128)(2,1)S(1)} async-done(((bf16[16,272,128]{2,1,0:T(8,128)(2,1)}), bf16[16,272,128]{2,1,0:T(8,128)(2,1)S(1)}, u32[]{:S(2)}, u32[]{:S(2)}) %all-to-all-start) | async-done | bytes 1114144 | tf_op jit(solution)/shard_map/all_to_all | solution.py:319
  92.3 14.5 %shard_map.103 = (bf16[2,2048,2048]{2,1,0:T(8,128)(2,1)}, bf16[2,128,2048]{2,1,0:T(8,128)(2,1)S(1)}) custom-call(bf16[16,272,128]{2,1,0:T(8,128)(2,1)S(1)} %all-to-all-done.x_ref), custom_call_target="tpu_custom_call" | custom-call | flops 1000000 | bytes 1000000 | tf_op jit(solution)/shard_map/pallas_call | solution.py:363
  106.8 6.6 %collective-permute-done.4.c_ref = bf16[608,128]{1,0:T(8,128)(2,1)S(1)} collective-permute-done((bf16[608,128]{1,0:T(8,128)(2,1)S(1)}, bf16[608,128]{1,0:T(8,128)(2,1)S(1)}, u32[]{:S(2)}, u32[]{:S(2)}) %collective-permute-start.4) | collective-permute-done | bytes 155680 | tf_op jit(solution)/shard_map/ppermute | solution.py:361
  113.4 1.2 shard_map.106
  114.5 1.0 copy-done.2
  115.5 0.7 copy-done.9
  116.2 0.8 copy-done.17
  116.9 7.2 %all-to-all-start.1 = ((bf16[16,32,128]{2,1,0:T(8,128)(2,1)}), bf16[16,32,128]{2,1,0:T(8,128)(2,1)}, u32[]{:S(2)}, u32[]{:S(2)}) async-start(bf16[16,32,128]{2,1,0:T(8,128)(2,1)} %get-tuple-element.59), calls=%async_computation.1 | async-start | bytes 262144 | tf_op jit(solution)/shard_map/all_to_all | solution.py:319
  124.2 1.6 copy-done.4
  125.8 1.4 copy-done.5
  127.6 10.9 %all-to-all-done.1.r_ref = bf16[16,32,128]{2,1,0:T(8,128)(2,1)} async-done(((bf16[16,32,128]{2,1,0:T(8,128)(2,1)}), bf16[16,32,128]{2,1,0:T(8,128)(2,1)}, u32[]{:S(2)}, u32[]{:S(2)}) %all-to-all-start.1) | async-done | bytes 131104 | tf_op jit(solution)/shard_map/all_to_all | solution.py:319
  138.5 2.5 shard_map.108
  141.1 0.7 copy-done.8
  143.0 16.2 %all-gather.3 = bf16[128,1408]{1,0:T(8,128)(2,1)S(1)} all-gather(bf16[32,1408]{1,0:T(8,128)(2,1)} %copy-done.13), channel_id=5, replica_groups={{0,1,2,3},{4,5,6,7},{8,9,10,11},{12,13,14,15},{16,17,18,19},{20,21,22,2..., dimensions={0}, use_global_device_ids=true | all-gather | bytes 450560 | tf_op jit(solution)/shard_map/all_gather | solution.py:323
  159.2 0.9 copy-done.10
  160.2 0.8 copy-done.15
  161.0 2.6 shard_map.109
  164.2 0.7 copy-done.12
  164.9 7.1 %all-to-all-start.2 = ((bf16[16,32,128]{2,1,0:T(8,128)(2,1)}), bf16[16,32,128]{2,1,0:T(8,128)(2,1)S(1)}, u32[]{:S(2)}, u32[]{:S(2)}) async-start(bf16[16,32,128]{2,1,0:T(8,128)(2,1)} %copy-done.11), calls=%async_computation.2 | async-start | bytes 262144 | tf_op jit(solution)/shard_map/all_to_all | solution.py:319
  172.0 11.2 %all-gather.4 = bf16[128,1920]{1,0:T(8,128)(2,1)S(1)} all-gather(bf16[32,1920]{1,0:T(8,128)(2,1)} %copy-done.12), channel_id=6, replica_groups={{0,4,8,12},{1,5,9,13},{2,6,10,14},{3,7,11,15},{16,20,24,28},{17,21,25,2..., dimensions={0}, use_global_device_ids=true | all-gather | bytes 614400 | tf_op jit(solution)/shard_map/all_gather | solution.py:323
  183.2 1.2 copy-done.6
  184.4 1.4 shard_map.110
  187.5 12.3 %all-to-all-start.3 = ((bf16[8,432,128]{2,1,0:T(8,128)(2,1)}), bf16[8,432,128]{2,1,0:T(8,128)(2,1)S(1)}, u32[]{:S(2)}, u32[]{:S(2)}) async-start(bf16[8,432,128]{2,1,0:T(8,128)(2,1)} %bitcast.5), calls=%async_computation.3 | async-start | bytes 1769472 | tf_op jit(solution)/shard_map/all_to_all | solution.py:319
  199.8 6.9 %collective-permute-start.6 = (bf16[4,128,128]{2,1,0:T(8,128)(2,1)S(1)}, bf16[4,128,128]{2,1,0:T(8,128)(2,1)S(1)}, u32[]{:S(2)}, u32[]{:S(2)}) collective-permute-start(bf16[4,128,128]{2,1,0:T(8,128)(2,1)S(1)} %copy-done.20), channel_id=1, source_target_pairs={{0,1},{1,2},{2,3},{3,0},{4,5},{5,6},{6,7},{7,4},{8,9},{9,10},{10,1... | collective-permute-start | bytes 393224 | tf_op jit(solution)/shard_map/ppermute | solution.py:442
  206.7 7.2 %collective-permute-start.7 = (bf16[4,128,128]{2,1,0:T(8,128)(2,1)S(1)}, bf16[4,128,128]{2,1,0:T(8,128)(2,1)S(1)}, u32[]{:S(2)}, u32[]{:S(2)}) collective-permute-start(bf16[4,128,128]{2,1,0:T(8,128)(2,1)S(1)} %get-tuple-element.77), channel_id=1, source_target_pairs={{0,2},{1,3},{2,0},{3,1},{4,6},{5,7},{6,4},{7,5},{8,10},{9,11},{10,... | collective-permute-start | bytes 393224 | tf_op jit(solution)/shard_map/ppermute | solution.py:442
  213.9 6.8 %collective-permute-start.8 = (bf16[4,128,128]{2,1,0:T(8,128)(2,1)S(1)}, bf16[4,128,128]{2,1,0:T(8,128)(2,1)S(1)}, u32[]{:S(2)}, u32[]{:S(2)}) collective-permute-start(bf16[4,128,128]{2,1,0:T(8,128)(2,1)S(1)} %get-tuple-element.78), channel_id=1, source_target_pairs={{0,3},{1,0},{2,1},{3,2},{4,7},{5,4},{6,5},{7,6},{8,11},{9,8},{10,9... | collective-permute-start | bytes 393224 | tf_op jit(solution)/shard_map/ppermute | solution.py:442
  220.8 1.0 copy-done.18
  221.8 15.5 %shard_map.112 = bf16[16,128,128]{2,1,0:T(8,128)(2,1)} custom-call(bf16[128,128]{1,0:T(8,128)(2,1)S(1)} %get-tuple-element.72.g_ref, bf16[16,272,128]{2,1,0:T(8,128)(2,1)S(1)} %copy-done.1, bf16[16,128,128]{2,1,0:T(8,128)(2,1)S(1)} %copy-done.18, bf16[2,2048,2048]{2,1,0:T(8,128)(2,1)} %get-tuple-element.74.p_ref), custom_call_target="tpu_custom_call" | custom-call | flops 10000000000 | bytes 20000000 | tf_op jit(solution)/shard_map/pallas_call | solution.py:443
  237.3 0.8 shard_map.113
  238.3 18.1 %all-gather.5 = bf16[1728,128]{1,0:T(8,128)(2,1)S(1)} all-gather(bf16[432,128]{1,0:T(8,128)(2,1)S(1)} %shard_map.114), channel_id=7, replica_groups={{0,32,64,96},{16,48,80,112},{128,160,192,224},{144,176,208,240},{256,28..., dimensions={0}, use_global_device_ids=true | all-gather | bytes 552960 | tf_op jit(solution)/shard_map/all_gather | solution.py:323
  256.4 5.7 %all-to-all-start.4 = ((bf16[16,128,128]{2,1,0:T(8,128)(2,1)}), bf16[16,128,128]{2,1,0:T(8,128)(2,1)S(1)}, u32[]{:S(2)}, u32[]{:S(2)}) async-start(bf16[16,128,128]{2,1,0:T(8,128)(2,1)} %shard_map.112), calls=%async_computation.4 | async-start | bytes 1048576 | tf_op jit(solution)/shard_map/all_to_all | solution.py:319
  262.2 18.4 %all-gather.7.r_ref = bf16[3456,128]{1,0:T(8,128)(2,1)S(1)} all-gather(bf16[432,128]{1,0:T(8,128)(2,1)S(1)} %shard_map.117), channel_id=9, replica_groups={{0,16,128,144,256,272,384,400},{32,48,160,176,288,304,416,432},{64,80,1..., dimensions={0}, use_global_device_ids=true | all-gather | bytes 995328 | tf_op jit(solution)/shard_map/all_gather | solution.py:323
  280.5 1.3 shard_map.118
  281.8 2.1 shard_map.115
  283.9 6.3 %all-to-all-done.4.r_ref = bf16[16,128,128]{2,1,0:T(8,128)(2,1)S(1)} async-done(((bf16[16,128,128]{2,1,0:T(8,128)(2,1)}), bf16[16,128,128]{2,1,0:T(8,128)(2,1)S(1)}, u32[]{:S(2)}, u32[]{:S(2)}) %all-to-all-start.4) | async-done | bytes 524320 | tf_op jit(solution)/shard_map/all_to_all | solution.py:319
  290.1 0.9 shard_map.116
  (55 shorter events, 4.6 us)
Async XLA Ops:
  7.2 109.8 %all-gather.15.cloned.1.call-start = ((), (), s32[]{:S(2)}) async-start(), calls=%async_computation.6 | async-start | bytes 1802240 | tf_op jit(solution)/shard_map/all_gather | solution.py:323
  10.1 19.3 %copy-start.7 = (bf16[1,128,2048]{2,1,0:T(8,128)(2,1)S(1)}, bf16[1,128,2048]{2,1,0:T(8,128)(2,1)}, u32[]{:S(2)}) copy-start(bf16[1,128,2048]{2,1,0:T(8,128)(2,1)} %v_ref) | copy-start | bytes 1572868
  10.1 44.1 %copy-start.16 = (bf16[1,8,1408]{2,1,0:T(8,128)(2,1)S(1)}, bf16[1,8,1408]{2,1,0:T(8,128)(2,1)}, u32[]{:S(2)}) copy-start(bf16[1,8,1408]{2,1,0:T(8,128)(2,1)} %teacher_ref) | copy-start | bytes 67588
  10.1 82.2 %all-to-all-start = ((bf16[16,272,128]{2,1,0:T(8,128)(2,1)}), bf16[16,272,128]{2,1,0:T(8,128)(2,1)S(1)}, u32[]{:S(2)}, u32[]{:S(2)}) async-start(bf16[16,272,128]{2,1,0:T(8,128)(2,1)} %shard_map.102), calls=%async_computation | async-start | bytes 2228224 | tf_op jit(solution)/shard_map/all_to_all | solution.py:319
  28.6 88.3 %all-gather.13.cloned.1.call-start = ((), (), s32[]{:S(2)}) async-start(), calls=%async_computation.5 | async-start | bytes 2621440 | tf_op jit(solution)/shard_map/all_gather | solution.py:323
  29.5 10.7 %collective-permute-start = (bf16[4,128,128]{2,1,0:T(8,128)(2,1)S(1)}, bf16[4,128,128]{2,1,0:T(8,128)(2,1)S(1)}, u32[]{:S(2)}, u32[]{:S(2)}) collective-permute-start(bf16[4,128,128]{2,1,0:T(8,128)(2,1)S(1)} %get-tuple-element.50), channel_id=1, source_target_pairs={{0,4},{1,5},{2,6},{3,7},{4,8},{5,9},{6,10},{7,11},{8,12},{9,13},{1... | collective-permute-start | bytes 393224 | tf_op jit(solution)/shard_map/ppermute | solution.py:353
  32.8 16.5 %collective-permute-start.1 = (bf16[4,128,128]{2,1,0:T(8,128)(2,1)S(1)}, bf16[4,128,128]{2,1,0:T(8,128)(2,1)S(1)}, u32[]{:S(2)}, u32[]{:S(2)}) collective-permute-start(bf16[4,128,128]{2,1,0:T(8,128)(2,1)S(1)} %get-tuple-element.51), channel_id=1, source_target_pairs={{0,8},{1,9},{2,10},{3,11},{4,12},{5,13},{6,14},{7,15},{8,0},{9,1},... | collective-permute-start | bytes 393224 | tf_op jit(solution)/shard_map/ppermute | solution.py:353
  37.1 17.1 %collective-permute-start.2 = (bf16[4,128,128]{2,1,0:T(8,128)(2,1)S(1)}, bf16[4,128,128]{2,1,0:T(8,128)(2,1)S(1)}, u32[]{:S(2)}, u32[]{:S(2)}) collective-permute-start(bf16[4,128,128]{2,1,0:T(8,128)(2,1)S(1)} %get-tuple-element.52), channel_id=1, source_target_pairs={{0,12},{1,13},{2,14},{3,15},{4,0},{5,1},{6,2},{7,3},{8,4},{9,5},{1... | collective-permute-start | bytes 393224 | tf_op jit(solution)/shard_map/ppermute | solution.py:353
  54.3 52.5 %collective-permute-start.3 = (bf16[608,128]{1,0:T(8,128)(2,1)S(1)}, bf16[608,128]{1,0:T(8,128)(2,1)S(1)}, u32[]{:S(2)}, u32[]{:S(2)}) collective-permute-start(bf16[608,128]{1,0:T(8,128)(2,1)S(1)} %get-tuple-element.55), channel_id=1, source_target_pairs={{0,1},{1,2},{2,3},{3,0},{4,5},{5,6},{6,7},{7,4},{8,9},{9,10},{10,1... | collective-permute-start | bytes 466952 | tf_op jit(solution)/shard_map/ppermute | solution.py:361
  61.3 52.1 %collective-permute-start.4 = (bf16[608,128]{1,0:T(8,128)(2,1)S(1)}, bf16[608,128]{1,0:T(8,128)(2,1)S(1)}, u32[]{:S(2)}, u32[]{:S(2)}) collective-permute-start(bf16[608,128]{1,0:T(8,128)(2,1)S(1)} %get-tuple-element.56), channel_id=1, source_target_pairs={{0,2},{1,3},{2,0},{3,1},{4,6},{5,7},{6,4},{7,5},{8,10},{9,11},{10,... | collective-permute-start | bytes 466952 | tf_op jit(solution)/shard_map/ppermute | solution.py:361
  70.1 43.3 %collective-permute-start.5 = (bf16[608,128]{1,0:T(8,128)(2,1)S(1)}, bf16[608,128]{1,0:T(8,128)(2,1)S(1)}, u32[]{:S(2)}, u32[]{:S(2)}) collective-permute-start(bf16[608,128]{1,0:T(8,128)(2,1)S(1)} %get-tuple-element.57), channel_id=1, source_target_pairs={{0,3},{1,0},{2,1},{3,2},{4,7},{5,4},{6,5},{7,6},{8,11},{9,8},{10,9... | collective-permute-start | bytes 466952 | tf_op jit(solution)/shard_map/ppermute | solution.py:361
  92.3 24.7 %copy-start = (bf16[16,272,128]{2,1,0:T(8,128)(2,1)}, bf16[16,272,128]{2,1,0:T(8,128)(2,1)S(1)}, u32[]{:S(2)}) copy-start(bf16[16,272,128]{2,1,0:T(8,128)(2,1)S(1)} %all-to-all-done.x_ref) | copy-start | bytes 3342340
  114.5 1.0 copy-start.2
  115.5 0.7 copy-start.9
  116.1 0.8 copy-start.17
  116.9 21.6 %all-to-all-start.1 = ((bf16[16,32,128]{2,1,0:T(8,128)(2,1)}), bf16[16,32,128]{2,1,0:T(8,128)(2,1)}, u32[]{:S(2)}, u32[]{:S(2)}) async-start(bf16[16,32,128]{2,1,0:T(8,128)(2,1)} %get-tuple-element.59), calls=%async_computation.1 | async-start | bytes 262144 | tf_op jit(solution)/shard_map/all_to_all | solution.py:319
  124.2 59.0 %all-gather.17.cloned.1.call-start = ((), (), s32[]{:S(2)}) async-start(), calls=%async_computation.7 | async-start | bytes 1351680 | tf_op jit(solution)/shard_map/all_gather | solution.py:323
  124.2 1.6 copy-start.4
  125.8 1.4 copy-start.5
  141.1 0.7 copy-start.8
  141.8 0.6 copy-start.13
  142.4 0.6 copy-start.14
  159.2 0.9 copy-start.10
  160.2 0.8 copy-start.15
  163.6 0.7 copy-start.11
  164.2 0.7 copy-start.12
  164.9 21.4 %all-to-all-start.2 = ((bf16[16,32,128]{2,1,0:T(8,128)(2,1)}), bf16[16,32,128]{2,1,0:T(8,128)(2,1)S(1)}, u32[]{:S(2)}, u32[]{:S(2)}) async-start(bf16[16,32,128]{2,1,0:T(8,128)(2,1)} %copy-done.11), calls=%async_computation.2 | async-start | bytes 262144 | tf_op jit(solution)/shard_map/all_to_all | solution.py:319
  172.0 14.3 %copy-start.3 = (bf16[2,128,2048]{2,1,0:T(8,128)(2,1)S(1)}, bf16[2,128,2048]{2,1,0:T(8,128)(2,1)}, u32[]{:S(2)}) copy-start(bf16[2,128,2048]{2,1,0:T(8,128)(2,1)} %copy-done.2) | copy-start | bytes 3145732
  183.2 1.2 copy-start.6
  185.8 35.0 %copy-start.1 = (bf16[16,272,128]{2,1,0:T(8,128)(2,1)S(1)}, bf16[16,272,128]{2,1,0:T(8,128)(2,1)}, u32[]{:S(2)}) copy-start(bf16[16,272,128]{2,1,0:T(8,128)(2,1)} %copy-done) | copy-start | bytes 3342340
  186.8 0.7 copy-start.19
  187.5 12.3 %copy-start.20 = (bf16[4,128,128]{2,1,0:T(8,128)(2,1)S(1)}, bf16[4,128,128]{2,1,0:T(8,128)(2,1)}, u32[]{:S(2)}) copy-start(bf16[4,128,128]{2,1,0:T(8,128)(2,1)} %copy-done.19) | copy-start | bytes 393220
  187.5 50.6 %all-to-all-start.3 = ((bf16[8,432,128]{2,1,0:T(8,128)(2,1)}), bf16[8,432,128]{2,1,0:T(8,128)(2,1)S(1)}, u32[]{:S(2)}, u32[]{:S(2)}) async-start(bf16[8,432,128]{2,1,0:T(8,128)(2,1)} %bitcast.5), calls=%async_computation.3 | async-start | bytes 1769472 | tf_op jit(solution)/shard_map/all_to_all | solution.py:319
  199.8 82.0 %all-gather.19.cloned.1.call-start = ((), (), s32[]{:S(2)}) async-start(), calls=%async_computation.8 | async-start | bytes 2621440 | tf_op jit(solution)/shard_map/all_gather | solution.py:323
  199.8 37.5 %collective-permute-start.6 = (bf16[4,128,128]{2,1,0:T(8,128)(2,1)S(1)}, bf16[4,128,128]{2,1,0:T(8,128)(2,1)S(1)}, u32[]{:S(2)}, u32[]{:S(2)}) collective-permute-start(bf16[4,128,128]{2,1,0:T(8,128)(2,1)S(1)} %copy-done.20), channel_id=1, source_target_pairs={{0,1},{1,2},{2,3},{3,0},{4,5},{5,6},{6,7},{7,4},{8,9},{9,10},{10,1... | collective-permute-start | bytes 393224 | tf_op jit(solution)/shard_map/ppermute | solution.py:442
  206.7 30.6 %collective-permute-start.7 = (bf16[4,128,128]{2,1,0:T(8,128)(2,1)S(1)}, bf16[4,128,128]{2,1,0:T(8,128)(2,1)S(1)}, u32[]{:S(2)}, u32[]{:S(2)}) collective-permute-start(bf16[4,128,128]{2,1,0:T(8,128)(2,1)S(1)} %get-tuple-element.77), channel_id=1, source_target_pairs={{0,2},{1,3},{2,0},{3,1},{4,6},{5,7},{6,4},{7,5},{8,10},{9,11},{10,... | collective-permute-start | bytes 393224 | tf_op jit(solution)/shard_map/ppermute | solution.py:442
  213.9 23.4 %collective-permute-start.8 = (bf16[4,128,128]{2,1,0:T(8,128)(2,1)S(1)}, bf16[4,128,128]{2,1,0:T(8,128)(2,1)S(1)}, u32[]{:S(2)}, u32[]{:S(2)}) collective-permute-start(bf16[4,128,128]{2,1,0:T(8,128)(2,1)S(1)} %get-tuple-element.78), channel_id=1, source_target_pairs={{0,3},{1,0},{2,1},{3,2},{4,7},{5,4},{6,5},{7,6},{8,11},{9,8},{10,9... | collective-permute-start | bytes 393224 | tf_op jit(solution)/shard_map/ppermute | solution.py:442
  220.8 1.0 copy-start.18
  256.4 33.8 %all-to-all-start.4 = ((bf16[16,128,128]{2,1,0:T(8,128)(2,1)}), bf16[16,128,128]{2,1,0:T(8,128)(2,1)S(1)}, u32[]{:S(2)}, u32[]{:S(2)}) async-start(bf16[16,128,128]{2,1,0:T(8,128)(2,1)} %shard_map.112), calls=%async_computation.4 | async-start | bytes 1048576 | tf_op jit(solution)/shard_map/all_to_all | solution.py:319
Sparse Core Ops, SparseCore 0:
  10.1 50.2 all-gather.14
  62.4 38.8 all-gather.12
  143.2 30.5 all-gather.16
  238.3 40.6 all-gather.18
